TPU v7x, 32 devices: a whole 2x2x4 slice. The times are simulated.
32 devices in a mesh: row: 8 (over y, x, core), col: 4 (over z).
Axes of the slice: x: 2, y: 2, z: 4, core: 2. Of those that a mesh axis runs over, the one named last changes fastest.
Arguments:
- tokens: bfloat16 [384, 8192], P('col', 'row'), may hold values from -6 to 6
- gate_weight: bfloat16 [8192, 29568], P('row', 'col'), may hold values from -0.0625 to 0.0625
- up_weight: bfloat16 [8192, 29568], P('row', 'col'), may hold values from -0.0625 to 0.0625
- gate_lower: bfloat16 [16, 8192, 64], P('col', 'row'), may hold values from -0.0625 to 0.0625
- up_lower: bfloat16 [16, 8192, 64], P('col', 'row'), may hold values from -0.0625 to 0.0625
- gate_upper: bfloat16 [16, 64, 29568], P('row', None, 'col'), may hold values from -0.21875 to 0.21875
- up_upper: bfloat16 [16, 64, 29568], P('row', None, 'col'), may hold values from -0.21875 to 0.21875
- outgoing: int32 [1], replicated, may hold values from 0 to 15
- incoming: int32 [1], replicated, may hold values from 0 to 15
Outputs:
- new_gate: bfloat16 [8192, 29568], P('row', 'col')
- new_up: bfloat16 [8192, 29568], P('row', 'col')
- hidden: bfloat16 [384, 29568], P('row', 'col')
All inputs are finite; a program needn't handle non-finite values.
Results may differ from a plain program's by a relative error of at most 0.0058.
Values may be sent and summed in bfloat16 or wider, within the bound.
No kernel may reach another device: no remote copies, remote signals or barrier semaphores. Data moves between devices by JAX's collectives and lax.ppermute only.
A program may use at most 192 MiB of HBM per device.

v0:
```python
import jax
import jax.numpy as jnp
from jax import lax
from jax.sharding import PartitionSpec as P


def broadcast(value, axis, root):
    mine = lax.axis_index(axis) == root
    return lax.psum(jnp.where(mine, value, jnp.zeros_like(value)), axis)


def lower_slot(stacked, ident):
    local = stacked.shape[1]
    chosen = lax.dynamic_index_in_dim(stacked, ident % local, 1, keepdims=False)
    return broadcast(chosen, "col", ident // local)


def upper_slot(stacked, ident):
    local = stacked.shape[1]
    chosen = lax.dynamic_index_in_dim(stacked, ident % local, 1, keepdims=False)
    return broadcast(chosen, "row", ident // local)


def merged(weight, low_old, low_new, up_old, up_new):
    delta = jnp.dot(low_new, up_new, preferred_element_type=jnp.float32) - jnp.dot(
        low_old, up_old, preferred_element_type=jnp.float32
    )
    return (weight.astype(jnp.float32) + delta).astype(jnp.bfloat16)


def body(
    tokens, gate_weight, up_weight, gate_lower, up_lower, gate_upper, up_upper, outgoing, incoming
):
    old = outgoing[0]
    new = incoming[0]
    lower_stack = jnp.stack([gate_lower, up_lower])
    upper_stack = jnp.stack([gate_upper, up_upper])
    lower_old = lower_slot(lower_stack, old)
    lower_new = lower_slot(lower_stack, new)
    upper_old = upper_slot(upper_stack, old)
    upper_new = upper_slot(upper_stack, new)
    new_gate = merged(gate_weight, lower_old[0], lower_new[0], upper_old[0], upper_new[0])
    new_up = merged(up_weight, lower_old[1], lower_new[1], upper_old[1], upper_new[1])
    gathered = lax.all_gather(tokens, "col", axis=0, tiled=True)
    width = new_gate.shape[1]
    gate_part = jnp.dot(gathered, new_gate, preferred_element_type=jnp.float32)
    up_part = jnp.dot(gathered, new_up, preferred_element_type=jnp.float32)
    summed = lax.psum_scatter(
        jnp.concatenate([gate_part, up_part], axis=1), "row", scatter_dimension=0, tiled=True
    )
    gate_sum = summed[:, :width]
    up_sum = summed[:, width:]
    hidden = (jax.nn.silu(gate_sum) * up_sum).astype(jnp.bfloat16)
    return (new_gate, new_up, hidden)


def solution(mesh):
    return jax.shard_map(
        body,
        mesh=mesh,
        in_specs=(
            P("col", "row"),
            P("row", "col"),
            P("row", "col"),
            P("col", "row", None),
            P("col", "row", None),
            P("row", None, "col"),
            P("row", None, "col"),
            P(),
            P(),
        ),
        out_specs=(P("row", "col"), P("row", "col"), P("row", "col")),
        check_vma=False,
    )
```

profile of v0, /device:TPU:0, one launch (start us, length us, event | category | flops | bytes accessed | tf_op | source)
XLA Modules:
  0.0 438.7 jit_solution(2624611396423456941)
XLA Ops:
  7.2 0.0 all-reduce.7.cloned.1.call-start
  8.6 1.9 fusion.10
  10.5 0.0 all-reduce.7.cloned.1.call-update
  10.6 0.0 all-reduce.5.cloned.1.call-start
  10.7 4.3 fusion.2
  15.0 0.0 copy-start.5
  15.0 0.0 all-reduce.5.cloned.1.call-update
  15.0 0.0 reduce-scatter.4.cloned.1.call-start
  15.1 0.9 copy-done.5
  15.9 27.4 %all_gather.3 = bf16[384,1024]{1,0:T(8,128)(2,1)S(1)} all-gather(bf16[96,1024]{1,0:T(8,128)(2,1)S(1)} %copy-done.5), channel_id=1, replica_groups=mesh['row'=8,'col'=4] {'col'}, dimensions={0}, use_global_device_ids=true | all-gather | bytes 983040 | tf_op jit(solution)/shard_map/all_gather | solution.py:44
  43.4 15.5 %all-reduce.7.cloned.1.call-done = (bf16[2,1024,64]{1,2,0:T(8,128)(2,1)}, bf16[2,1024,64]{1,2,0:T(8,128)(2,1)}) async-done(((bf16[2,1024,64]{1,2,0:T(8,128)(2,1)}, bf16[2,1024,64]{1,2,0:T(8,128)(2,1)}), (bf16[2,1024,64]{1,2,0:T(8,128)(2,1)}, bf16[2,1024,64]{1,2,0:T(8,128)(2,1)})) %all-reduce.7.cloned.1.call-update) | async-done | bytes 524304 | tf_op jit(solution)/shard_map/psum | solution.py:9
  58.8 80.8 %all-reduce.5.cloned.1.call-done = (bf16[2,64,7392]{2,1,0:T(8,128)(2,1)}, bf16[2,64,7392]{2,1,0:T(8,128)(2,1)}) async-done(((bf16[2,64,7392]{2,1,0:T(8,128)(2,1)}, bf16[2,64,7392]{2,1,0:T(8,128)(2,1)}), (bf16[2,64,7392]{2,1,0:T(8,128)(2,1)}, bf16[2,64,7392]{2,1,0:T(8,128)(2,1)})) %all-reduce.5.cloned.1.call-update) | async-done | bytes 3784720 | tf_op jit(solution)/shard_map/psum | solution.py:9
  139.6 0.0 copy-start.2
  139.6 0.0 copy-start.4
  139.6 15.5 %fusion.6 = f32[1024,7392]{0,1:T(8,128)} fusion(bf16[2,64,7392]{2,1,0:T(8,128)(2,1)} %get-tuple-element.9, bf16[2,1024,64]{1,2,0:T(8,128)(2,1)} %get-tuple-element.11), kind=kOutput, calls=%fused_computation.22 | convolution fusion | flops 968884224 | bytes 31358976 | tf_op jit(solution)/shard_map/dot_general | solution.py:25
  155.1 0.0 copy-done.2
  155.1 0.0 copy-done.4
  155.1 0.0 copy-start.1
  155.1 0.0 copy-start.3
  155.1 12.2 %fusion.7 = f32[1024,7392]{0,1:T(8,128)} fusion(bf16[2,64,7392]{2,1,0:T(8,128)(2,1)S(1)} %copy-done.2, bf16[2,1024,64]{1,2,0:T(8,128)(2,1)S(1)} %copy-done.4), kind=kOutput, calls=%fused_computation.25 | convolution fusion | flops 968884224 | bytes 31358976 | tf_op jit(solution)/shard_map/dot_general | solution.py:25
  167.4 0.0 copy-done.1
  167.4 0.0 copy-done.3
  167.4 21.6 %add_convert_fusion = bf16[1024,7392]{0,1:T(8,128)(2,1)} fusion(f32[1024,7392]{0,1:T(8,128)} %fusion.6, bf16[1024,7392]{0,1:T(8,128)(2,1)} %param.11, bf16[2,64,7392]{2,1,0:T(8,128)(2,1)S(1)} %copy-done.1, bf16[2,1024,64]{1,2,0:T(8,128)(2,1)S(1)} %copy-done.3), kind=kOutput, calls=%fused_computation | convolution fusion | flops 999161856 | bytes 61636608 | tf_op jit(solution)/shard_map/dot_general | solution.py:25
  189.0 14.0 %convolution_bitcast_fusion = f32[384,7392]{0,1:T(8,128)} fusion(bf16[1024,7392]{0,1:T(8,128)(2,1)} %add_convert_fusion, bf16[384,1024]{1,0:T(8,128)(2,1)S(1)} %all_gather.3), kind=kOutput, calls=%fused_computation.3 | convolution fusion | flops 5813305344 | bytes 27279360 | tf_op jit(solution)/shard_map/dot_general | solution.py:47
  202.9 21.6 %add_convert_fusion.1 = bf16[1024,7392]{0,1:T(8,128)(2,1)} fusion(f32[1024,7392]{0,1:T(8,128)} %fusion.7, bf16[1024,7392]{0,1:T(8,128)(2,1)} %param.10, bf16[2,64,7392]{2,1,0:T(8,128)(2,1)S(1)} %copy-done.1, bf16[2,1024,64]{1,2,0:T(8,128)(2,1)S(1)} %copy-done.3), kind=kOutput, calls=%fused_computation.1 | convolution fusion | flops 999161856 | bytes 61636608 | tf_op jit(solution)/shard_map/dot_general | solution.py:25
  224.5 0.0 copy-start
  224.5 11.4 %convolution_bitcast_fusion.1 = f32[384,7392]{0,1:T(8,128)S(1)} fusion(bf16[1024,7392]{0,1:T(8,128)(2,1)} %add_convert_fusion.1, bf16[384,1024]{1,0:T(8,128)(2,1)S(1)} %all_gather.3), kind=kOutput, calls=%fused_computation.4 | convolution fusion | flops 5813305344 | bytes 27279360 | tf_op jit(solution)/shard_map/dot_general | solution.py:46
  235.9 0.0 copy-done
  235.9 14.5 %pad_maximum_fusion = f32[384,14784]{0,1:T(8,128)} fusion(f32[384,7392]{0,1:T(8,128)S(1)} %copy-done, f32[384,7392]{0,1:T(8,128)S(1)} %convolution_bitcast_fusion.1), kind=kLoop, calls=%fused_computation.2 | loop fusion | flops 5677056 | bytes 45416448 | tf_op jit(solution)/shard_map/concatenate | solution.py:49
  250.5 23.5 %copy.14 = f32[384,14784]{1,0:T(8,128)} copy(f32[384,14784]{0,1:T(8,128)} %pad_maximum_fusion) | data formatting | bytes 45416448
  274.0 0.0 reduce-scatter.4.cloned.1.call-update
  274.0 144.7 %reduce-scatter.4.cloned.1.call-done = f32[48,14784]{1,0:T(8,128)} async-done(((f32[384,14784]{1,0:T(8,128)}), f32[48,14784]{1,0:T(8,128)}) %reduce-scatter.4.cloned.1.call-update) | async-done | bytes 2838544
  418.7 2.2 fusion.14
  420.9 2.6 copy.16
  423.5 2.5 copy.17
  426.0 4.2 multiply_convert_fusion
  430.2 1.9 copy.13
Async XLA Ops:
  7.2 51.7 %all-reduce.7.cloned.1.call-start = ((), (), s32[]{:S(2)}) async-start(), calls=%async_computation.3 | async-start | bytes 1048576 | tf_op jit(solution)/shard_map/psum | solution.py:9
  10.6 129.1 %all-reduce.5.cloned.1.call-start = ((), (), s32[]{:S(2)}) async-start(), calls=%async_computation.2 | async-start | bytes 7602176 | tf_op jit(solution)/shard_map/psum | solution.py:9
  15.0 0.9 copy-start.5
  15.0 403.6 %reduce-scatter.4.cloned.1.call-start = ((), (), s32[]{:S(2)}) async-start(), calls=%async_computation.1 | async-start | bytes 25657344
  139.6 15.5 %copy-start.2 = (bf16[2,64,7392]{2,1,0:T(8,128)(2,1)S(1)}, bf16[2,64,7392]{2,1,0:T(8,128)(2,1)}, u32[]{:S(2)}) copy-start(bf16[2,64,7392]{2,1,0:T(8,128)(2,1)} %get-tuple-element.9) | copy-start | bytes 5677060
  139.6 15.5 %copy-start.4 = (bf16[2,1024,64]{1,2,0:T(8,128)(2,1)S(1)}, bf16[2,1024,64]{1,2,0:T(8,128)(2,1)}, u32[]{:S(2)}) copy-start(bf16[2,1024,64]{1,2,0:T(8,128)(2,1)} %get-tuple-element.11) | copy-start | bytes 786436
  155.1 12.3 %copy-start.1 = (bf16[2,64,7392]{2,1,0:T(8,128)(2,1)S(1)}, bf16[2,64,7392]{2,1,0:T(8,128)(2,1)}, u32[]{:S(2)}) copy-start(bf16[2,64,7392]{2,1,0:T(8,128)(2,1)} %get-tuple-element.10) | copy-start | bytes 5677060
  155.1 12.2 %copy-start.3 = (bf16[2,1024,64]{1,2,0:T(8,128)(2,1)S(1)}, bf16[2,1024,64]{1,2,0:T(8,128)(2,1)}, u32[]{:S(2)}) copy-start(bf16[2,1024,64]{1,2,0:T(8,128)(2,1)} %get-tuple-element.12) | copy-start | bytes 786436
  224.5 11.4 %copy-start = (f32[384,7392]{0,1:T(8,128)S(1)}, f32[384,7392]{0,1:T(8,128)}, u32[]{:S(2)}) copy-start(f32[384,7392]{0,1:T(8,128)} %convolution_bitcast_fusion) | copy-start | bytes 34062340
Sparse Core Ops, SparseCore 0:
  11.0 47.8 all-reduce.6
  62.8 76.7 all-reduce.4
  274.1 144.5 reduce-scatter.3
where the time goes:
time: 439 us
  waiting for transfers between devices  241 us (55%)
  matrix products  96.3 us (22%)
  local copies, waits for them, and re-layouts  33.6 us (8%)
  blocking collectives  27.4 us (6%)
  other arithmetic  25.1 us (6%)
  between operations  15.2 us (3%)
    unnamed x4, waiting for transfers between devices  145 us
    psum x2, waiting for transfers between devices, broadcast(): return lax.psum(jnp.where(mine, value, jnp.zeros_like(value)), axis)  96.2 us
    dot_general x2, matrix products, merged(): jnp.dot(low_old, up_old, preferred_element_type=jnp.float32)  43.2 us
    unnamed x16, local copies, waits for them, and re-layouts  31.4 us
    dot_general x2, matrix products, merged(): jnp.dot(low_new, up_new, preferred_element_type=jnp.float32)  27.7 us
    all_gather x1, blocking collectives, body(): gathered = lax.all_gather(tokens, 'col', axis=0, tiled=True)  27.4 us
    concatenate x1, other arithmetic, body(): jnp.concatenate([gate_part, up_part], axis=1)  14.5 us
    dot_general x1, matrix products, body(): up_part = jnp.dot(gathered, new_up, preferred_element_type=jnp.float32)  14 us
  transfers between devices with their start and end apart: 3, of which 3 were waited for; matrix products, arithmetic and copies ran while one was open for 1% of the time, Pallas kernels for 0%

commit v1 on v0

v1 whole, which is shorter than its diff:
```python
import functools

import jax
import jax.numpy as jnp
from jax import lax
from jax.experimental import pallas as pl
from jax.experimental.pallas import tpu as pltpu
from jax.sharding import PartitionSpec as P

TILE = 512
SUB = 256
CHUNKS = 3
F32 = jnp.float32
BF16 = jnp.bfloat16
SMALL = pl.CostEstimate(flops=1024, bytes_accessed=1024, transcendentals=0)
COST = pl.CostEstimate(flops=2**34, bytes_accessed=2**25, transcendentals=0)
VMEM = pl.BlockSpec(memory_space=pltpu.VMEM)


def after(value, others):
    return lax.optimization_barrier((value, others))[0]


def bit(value, which):
    return (value >> which) & 1


def swap(value, axis, size, distance):
    return lax.ppermute(value, axis, [(i, i ^ distance) for i in range(size)])


def block_order(bits):
    offsets = range(0, 2 ** (len(bits) + 1), 2)
    return sorted(offsets, key=lambda k: tuple(-bit(k, b) for b in bits))


class Factor:
    def __init__(self, axis, size, index, bits, held, sent, owner):
        self.axis, self.size, self.index, self.bits = axis, size, index, bits
        self.held, self.owner = held, owner
        self.arrived = [swap(sent, axis, size, 1 << bits[0])]
        self.last = bits[0]
        self.todo = [("scatter", b) for b in bits[1:]] + [("turn", bits[-1])]
        self.todo += [("gather", b) for b in reversed(bits[:-1])]

    def chosen(self):
        mine = bit(self.index, self.last)
        return jnp.where(mine == bit(self.owner, self.last), self.held, self.arrived[0])

    def joined(self):
        low = jnp.concatenate([self.held, self.arrived[0]], axis=0)
        high = jnp.concatenate([self.arrived[0], self.held], axis=0)
        return jnp.where(bit(self.index, self.last) == 0, low, high)

    def step(self):
        kind, b = self.todo.pop(0)
        if kind == "scatter":
            value = self.chosen()
            half = value.shape[0] // 2
            mine = bit(self.index, b)
            sent = lax.dynamic_slice_in_dim(value, (1 - mine) * half, half, 0)
            self.held = lax.dynamic_slice_in_dim(value, mine * half, half, 0)
        else:
            self.held = sent = self.chosen() if kind == "turn" else self.joined()
        self.arrived = [swap(sent, self.axis, self.size, 1 << b)]
        self.last = b
        return sent


def tokens_kernel(rows, at, *refs):
    first = 0
    for ref in refs[:-1]:
        for h in range(ref.shape[0] // rows):
            start = pl.multiple_of(at[first + h] * rows, rows)
            refs[-1][pl.ds(start, rows), :] = ref[h * rows : (h + 1) * rows, :]
        first += ref.shape[0] // rows


def ordered_tokens(parts, offsets, n_row, row, col, bits):
    rows = sum(part.shape[0] for part in parts) // n_row
    blocks = n_row // len(offsets)
    source = (col ^ jnp.array(offsets, jnp.int32))[:, None]
    offset = ((source * blocks + jnp.arange(blocks, dtype=jnp.int32)) ^ row).reshape(-1)
    place = offset * 0
    for b in [0] + bits:
        place = place * 2 + 1 - bit(offset, b)
    return pl.pallas_call(
        functools.partial(tokens_kernel, rows),
        out_shape=jax.ShapeDtypeStruct((rows * n_row, parts[0].shape[1]), BF16),
        in_specs=[pl.BlockSpec(memory_space=pltpu.SMEM)] + [VMEM] * len(parts),
        out_specs=VMEM,
        compiler_params=pltpu.CompilerParams(vmem_limit_bytes=12 * 2**20),
        name="order_tokens",
    )(place, *parts)


def times_transposed(left, right):
    return lax.dot_general(left, right, (((1,), (1,)), ((), ())), preferred_element_type=F32)


def multiply_kernel(rows, places, tok, gate_w, up_w, away, gate_home, up_home):
    half = tok.shape[0] // 2
    part = times_transposed(tok[...], gate_w[...])
    away[:half, :] = part[:half].astype(BF16)
    gate_home[...] = part[half:]
    part = times_transposed(tok[...], up_w[...])
    for to, at in enumerate(places):
        into = slice(to * rows, (to + 1) * rows)
        away[half + to * rows : half + (to + 1) * rows, :] = part[at * rows :][:rows].astype(BF16)
        up_home[into, :] = part[half + at * rows :][:rows]


def multiply_chunk(span, columns, weights, tok, rows, places):
    first, count = span
    n_tok, depth = tok.shape
    half = n_tok // 2
    weight = pl.BlockSpec((TILE, depth), lambda i: (first + i, 0))
    return pl.pallas_call(
        functools.partial(multiply_kernel, rows, places),
        grid=(count,),
        out_shape=[
            jax.ShapeDtypeStruct((n_tok, columns), BF16),
            jax.ShapeDtypeStruct((half, columns), F32),
            jax.ShapeDtypeStruct((half, columns), F32),
        ],
        in_specs=[pl.BlockSpec(tok.shape, lambda i: (0, 0)), weight, weight],
        out_specs=[
            pl.BlockSpec((n_tok, TILE), lambda i: (0, i)),
            pl.BlockSpec((half, TILE), lambda i: (0, i)),
            pl.BlockSpec((half, TILE), lambda i: (0, i)),
        ],
        compiler_params=pltpu.CompilerParams(
            dimension_semantics=("arbitrary",), vmem_limit_bytes=40 * 2**20
        ),
        cost_estimate=COST,
        name="multiply",
    )(tok, *weights)


def lower_kernel(rows, places, tok, low, old_away, old_gate, old_up, away, gate_home, up_home):
    rank = low.shape[0] // 2
    multiply_kernel(
        rows, places, tok, low.at[:rank, :], low.at[rank:, :], away, gate_home, up_home
    )


def multiply_lower(tok, low, part, rows, places):
    rank = low.shape[0] // 2
    last = part[0].shape[1] // rank - 1
    specs = [pl.BlockSpec((array.shape[0], rank), lambda i: (0, last)) for array in part]
    return pl.pallas_call(
        functools.partial(lower_kernel, rows, places),
        grid=(1,),
        out_shape=[jax.ShapeDtypeStruct(array.shape, array.dtype) for array in part],
        in_specs=[pl.BlockSpec(array.shape, lambda i: (0, 0)) for array in (tok, low)] + specs,
        out_specs=specs,
        input_output_aliases={2: 0, 3: 1, 4: 2},
        compiler_params=pltpu.CompilerParams(vmem_limit_bytes=12 * 2**20),
        cost_estimate=SMALL,
        name="multiply_lower",
    )(tok, low, *part)


def merge_kernel(low, gate_w, up_w, gate_b, gate_c, up_b, up_c, *refs):
    rank = gate_b.shape[0]
    for start in range(0, TILE, SUB):
        units = slice(start, start + SUB)
        for t, (weight, mine, other) in enumerate(
            ((gate_w, gate_b, gate_c), (up_w, up_b, up_c))
        ):
            delta = lax.dot_general(
                jnp.concatenate([mine[:, units], other[:, units]], axis=0),
                low[2 * t * rank : 2 * (t + 1) * rank, :],
                (((0,), (0,)), ((), ())),
                preferred_element_type=F32,
            )
            refs[t - 2][units, :] = (weight[units, :].astype(F32) + delta).astype(BF16)


def merge_span(span, weights, low, uppers, merged):
    first, count = span
    units, depth = weights[0].shape
    weight = pl.BlockSpec((TILE, depth), lambda i: (first + i, 0))
    upper = pl.BlockSpec((uppers[0].shape[0], TILE), lambda i: (0, first + i))
    operands = [low, *weights, *uppers, *merged]
    specs = [pl.BlockSpec(low.shape, lambda i: (0, 0)), weight, weight] + [upper] * 4
    specs += [pl.BlockSpec(memory_space=pl.ANY)] * len(merged)
    return pl.pallas_call(
        merge_kernel,
        grid=(count,),
        out_shape=[jax.ShapeDtypeStruct((units, depth), BF16)] * 2,
        in_specs=specs,
        out_specs=[weight] * 2,
        input_output_aliases={7: 0, 8: 1} if merged else {},
        compiler_params=pltpu.CompilerParams(
            dimension_semantics=("arbitrary",), vmem_limit_bytes=40 * 2**20
        ),
        cost_estimate=SMALL,
        name="merge",
    )(*operands)


class Sum:
    def __init__(self, away, gate, up, n_row):
        half = gate.shape[0]
        self.home = [gate, up]
        self.arrived = [swap(away, "row", n_row, 1)]
        self.places = [(0, 0, half), (0, half, half)]
        self.step = 0

    def came(self, t):
        array, start, size = self.places[t]
        return self.arrived[array][start : start + size].astype(F32)

    def finish(self):
        return [self.home[t] + self.came(t) for t in range(2)]


def exchange(items, orders, n_row):
    groups = {}
    for item in items:
        for t in range(2):
            home, came = item.home[t], item.came(t)
            half = home.shape[0] // 2
            groups.setdefault(orders[t][item.step], []).append(
                (item, t, (home[:half] + came[:half]).astype(BF16))
            )
            item.home[t] = home[half:] + came[half:]
    arrived, sent = [], []
    for number, (b, members) in enumerate(sorted(groups.items())):
        sent.append(jnp.concatenate([rows for _, _, rows in members], axis=0))
        arrived.append(swap(sent[-1], "row", n_row, 1 << b))
        start = 0
        for item, t, rows in members:
            item.places[t] = (number, start, rows.shape[0])
            start += rows.shape[0]
    for item in items:
        item.arrived = arrived
        item.step += 1
    return sent


def finish_kernel(gate_home, gate_came, up_home, up_came, sums, gate_b, gate_c, up_b, up_c, *refs):
    rank = 2 * gate_b.shape[0]
    high = sums[...].astype(BF16)
    low = (sums[...] - high.astype(F32)).astype(BF16)

    def total(home, came, mine, other, units, columns):
        upper = jnp.concatenate([mine[:, units], other[:, units]], axis=0)
        value = home[:, units] + came[:, units].astype(F32)
        for part in (high, low):
            value += jnp.dot(part[:, columns], upper, preferred_element_type=F32)
        return value

    for start in range(0, gate_home.shape[1], TILE):
        units = slice(start, start + TILE)
        gate = total(gate_home, gate_came, gate_b, gate_c, units, slice(0, rank))
        up = total(up_home, up_came, up_b, up_c, units, slice(rank, 2 * rank))
        refs[-1][:, units] = (jax.nn.silu(gate) * up).astype(BF16)


def finished(number, item, sums, uppers, units, hidden):
    rows, columns = item.home[0].shape
    home = pl.BlockSpec((rows, columns), lambda i: (0, 0))
    upper = pl.BlockSpec((uppers[0].shape[0], columns), lambda i: (0, number))
    operands, specs = [], []
    for t in range(2):
        array, start, _ = item.places[t]
        block = start // rows
        operands += [item.home[t], item.arrived[array]]
        specs += [home, pl.BlockSpec((rows, columns), lambda i, block=block: (block, 0))]
    operands += [sums, *uppers, *hidden]
    specs += [pl.BlockSpec(sums.shape, lambda i: (0, 0))] + [upper] * 4
    specs += [pl.BlockSpec(memory_space=pl.ANY)] * len(hidden)
    return pl.pallas_call(
        finish_kernel,
        grid=(1,),
        out_shape=[jax.ShapeDtypeStruct((rows, units), BF16)],
        in_specs=specs,
        out_specs=[pl.BlockSpec((rows, columns), lambda i: (0, number))],
        input_output_aliases={9: 0} if hidden else {},
        compiler_params=pltpu.CompilerParams(vmem_limit_bytes=14 * 2**20),
        name="finish",
    )(*operands)


def body(
    n_row, n_col, tokens, gate_weight, up_weight, gate_lower, up_lower, gate_upper, up_upper,
    outgoing, incoming,
):
    old, new = outgoing[0], incoming[0]
    row, col = lax.axis_index("row"), lax.axis_index("col")
    core = bit(row, 0)
    others = list(range(1, n_row.bit_length() - 1))
    orders = [others, others[1:] + others[:1]]
    stages = len(others)
    weights = [gate_weight.T, up_weight.T]
    units = weights[0].shape[0]
    rank = gate_upper.shape[1]
    tiles = pl.cdiv(pl.cdiv(units, 2 * rank) * 2 * rank + 2 * rank, TILE)
    per = pl.cdiv(tiles, CHUNKS)
    spans = [(first, min(per, tiles - first)) for first in range(0, tiles, per)]
    turns = list(range(len(spans)))
    turns[1:] = turns[:0:-1]
    used = pl.cdiv(units, TILE)

    state, sums = {"sent": []}, {}
    col_bits = list(range(n_col.bit_length() - 1))
    def slots(near, local):
        keep, other = jnp.where(near == 0, new, old), jnp.where(near == 0, old, new)
        return keep // local, [keep % local, other % local]

    upper_owner, upper_at = slots(bit(row, 0), gate_upper.shape[0])
    lower_owner, lower_at = slots(bit(col, 0), gate_lower.shape[0])

    def slot(stack, i):
        return lax.dynamic_index_in_dim(stack, i, 0, keepdims=False)

    offsets = [0]
    gathered = [swap(tokens, "col", n_col, 1 << col_bits[-1])]
    lowers = jnp.concatenate([jnp.swapaxes(a, 1, 2) for a in (gate_lower, up_lower)], axis=1)
    lower = Factor(
        "col", n_col, col, col_bits, *[slot(lowers, i) for i in lower_at], lower_owner
    )
    uppers = [
        Factor(
            "row", n_row, row, [0] + order, *[slot(stack, i) for i in upper_at], upper_owner
        )
        for stack, order in zip((gate_upper, up_upper), orders)
    ]

    def fence(*arrivals):
        items = list(sums.values())
        values = (
            state, [f.held for f in uppers + [lower]], [item.home for item in items],
            [item.arrived for item in arrivals],
        )
        values = lax.optimization_barrier(values)
        state.update(values[0])
        for factor, held in zip(uppers + [lower], values[1]):
            factor.held = held
        for item, home in zip(items, values[2]):
            item.home = home
        for item, arrived in zip(arrivals, values[3]):
            item.arrived = arrived

    def forward(*factors):
        state["sent"] = [state["sent"], [f.step() for f in factors if f.todo]]

    def running():
        return [f for f in uppers + [lower] if f.todo]

    def step():
        items = [sums[turn] for turn in turns if turn in sums]
        ready = [
            item for i, item in enumerate(items)
            if item.step < stages and (i == 0 or items[i - 1].step > item.step)
        ]
        if ready:
            state["sent"] = exchange(ready, orders, n_row)
        return ready

    for number, b in enumerate(reversed(col_bits)):
        fence()
        parts = [state.pop("parts", tokens)] + gathered
        offsets = offsets + [o ^ (1 << b) for o in offsets]
        if number + 1 < len(col_bits):
            state["parts"] = jnp.concatenate(parts, axis=0)
            gathered = [swap(state["parts"], "col", n_col, 1 << (b - 1))]
            forward(*uppers if number == 0 else (), lower)
    tok = state["tok"] = ordered_tokens(parts, offsets, n_row, row, col, orders[0])
    fence()
    forward(*uppers, lower)
    fence()

    rows = tok.shape[0] // n_row
    columns = per * TILE
    places = [block_order(orders[0]).index(k) for k in block_order(orders[1])]

    def low_factors():
        value = lower.joined()
        half = value.shape[0] // 2
        fresh, stale = value[:half], value[half:]
        return jnp.concatenate([fresh[:rank], -stale[:rank], fresh[rank:], -stale[rank:]], axis=0)

    flying = []
    for number, turn in enumerate(turns):
        part = multiply_chunk(spans[turn], columns, weights, state["tok"], rows, places)
        state["part"] = part
        fence(*running() if number < 2 else ())
        if number == 1 or len(turns) == 1:
            while lower.todo:
                forward(lower)
            state["low"] = low_factors()
            state["part"] = multiply_lower(state["tok"], state["low"], state["part"], rows, places)
        sums[turn] = Sum(*state.pop("part"), n_row)
        if number < 2:
            forward(*running())
        if number == 0:
            fence(sums[turn])
            flying = step()
        fence()
    fence(*flying, *[sums[turn] for turn in turns[1:2]])
    flying = step()
    fence()
    while running():
        fence(*uppers)
        forward(*uppers)
    fence(*uppers)

    def by_core(value, axis):
        parts = jnp.split(value, 4, axis=axis)
        turned = [parts[i] for i in (1, 0, 3, 2)]
        return jnp.where(
            core == 0, jnp.concatenate(parts, axis=axis), jnp.concatenate(turned, axis=axis)
        )

    state["uppers"] = [part for f in uppers for part in (f.held, f.arrived[0])]
    state["low"] = by_core(state["low"], 0)
    fence()
    cuts = [0, used * 2 // 5, used * 4 // 5, used]
    state["merged"] = []
    done = 0
    for first, last in zip(cuts, cuts[1:]):
        state["merged"] = merge_span(
            (first, last - first), weights, state["low"], state["uppers"], state["merged"]
        )
        fence(*flying, *[sums[turn] for turn in turns[2:] if sums[turn].step == 0])
        flying = step()
        fence()
    while flying:
        flying = step()

    ends = sums[turns[min(1, len(turns) - 1)]].finish()
    correction = jnp.concatenate([end[:, columns - 2 * rank :] for end in ends], axis=1)
    correction = by_core(correction, 1)
    hidden = []
    for turn in turns:
        hidden = finished(turn, sums[turn], correction, state["uppers"], units, hidden)
    merged = state["merged"]
    return merged[0].T, merged[1].T, hidden[0]


def solution(mesh):
    return jax.shard_map(
        functools.partial(body, mesh.shape["row"], mesh.shape["col"]),
        mesh=mesh,
        in_specs=(
            P("col", "row"),
            P("row", "col"),
            P("row", "col"),
            P("col", "row", None),
            P("col", "row", None),
            P("row", None, "col"),
            P("row", None, "col"),
            P(),
            P(),
        ),
        out_specs=(P("row", "col"), P("row", "col"), P("row", "col")),
        check_vma=False,
    )
```

time: 439 us -> 128 us (0.29)
  waiting for transfers between devices: 241 us -> 21.5 us
  matrix products: 96.3 us -> 0 us
  Pallas kernels: 0 us -> 57.9 us
  starting transfers between devices: 0.12 us -> 30 us
  blocking collectives: 27.4 us -> 0 us
  local copies, waits for them, and re-layouts: 33.6 us -> 6.74 us
  other arithmetic: 25.1 us -> 7.66 us
  between operations: 15.2 us -> 2.53 us
    unnamed x4 -> x0, waiting for transfers between devices: 145 us -> none
    dot_general x6 -> x0, matrix products: 96.3 us -> none  [the longest x2 43.2 us: merged(): jnp.dot(low_old, up_old, preferred_element_type=jnp.float32)]
    psum x2 -> x0, waiting for transfers between devices: 96.2 us -> none  [broadcast(): return lax.psum(jnp.where(mine, value, jnp.zeros_like(value)), axis)]
    pallas_call x0 -> x11, Pallas kernels: none -> 57.9 us  [the longest x3 29.8 us: merge_span(): pl.pallas_call(merge_kernel, grid=(count,), out_shape=[jax.ShapeDtypeStru...]
    unnamed x16 -> x3, local copies, waits for them, and re-layouts: 31.4 us -> 0.95 us
    ppermute x0 -> x29, starting transfers between devices: none -> 30 us  [swap(): return lax.ppermute(value, axis, [(i, i ^ distance) for i in range(size)])]
    all_gather x1 -> x0, blocking collectives: 27.4 us -> none  [body(): gathered = lax.all_gather(tokens, 'col', axis=0, tiled=True)]
    ppermute x0 -> x29, waiting for transfers between devices: none -> 21.5 us  [swap(): return lax.ppermute(value, axis, [(i, i ^ distance) for i in range(size)])]
  transfers between devices with their start and end apart: 3 -> 29, of which waited for: 3 -> 11; matrix products, arithmetic and copies ran while one was open for 1% -> 10% of each run, Pallas kernels for 0% -> 43%
where the time goes in v1:
time: 128 us; the launch traced here: 126 us
  Pallas kernels  57.9 us (45%)
  starting transfers between devices  30 us (23%)
  waiting for transfers between devices  21.5 us (17%)
  other arithmetic  7.66 us (6%)
  local copies, waits for them, and re-layouts  6.74 us (5%)
  between operations  2.53 us (2%)
    ppermute x29, starting transfers between devices, swap(): return lax.ppermute(value, axis, [(i, i ^ distance) for i in range(size)])  30 us
    pallas_call x3, Pallas kernels, merge_span(): pl.pallas_call(merge_kernel, grid=(count,), out_shape=[jax.ShapeDtypeStru...  29.8 us
    pallas_call x3, Pallas kernels, multiply_chunk(): pl.pallas_call(functools.partial(multiply_kernel, rows, places), grid=(co...  23.4 us
    ppermute x29, waiting for transfers between devices, swap(): return lax.ppermute(value, axis, [(i, i ^ distance) for i in range(size)])  21.5 us
    squeeze x2, local copies, waits for them, and re-layouts, slot(): return lax.dynamic_index_in_dim(stack, i, 0, keepdims=False)  4.32 us
    pallas_call x3, Pallas kernels, finished(): pl.pallas_call(finish_kernel, grid=(1,), out_shape=[jax.ShapeDtypeStruct(...  3.55 us
  transfers between devices with their start and end apart: 29, of which 11 were waited for; matrix products, arithmetic and copies ran while one was open for 10% of the time, Pallas kernels for 43%

profile of v1, /device:TPU:0, one launch (start us, length us, event | category | flops | bytes accessed | tf_op | source)
XLA Modules:
  0.0 126.3 jit_solution(1113003445966243967)
XLA Ops:
  0.6 4.1 %collective-permute-start = (bf16[96,1024]{1,0:T(8,128)(2,1)}, bf16[96,1024]{1,0:T(8,128)(2,1)}, u32[]{:S(2)}, u32[]{:S(2)}) collective-permute-start(bf16[96,1024]{1,0:T(8,128)(2,1)} %param.10), channel_id=1, source_target_pairs={{0,2},{1,3},{2,0},{3,1},{4,6},{5,7},{6,4},{7,5},{8,10},{9,11},{10,... | collective-permute-start | bytes 589832 | tf_op jit(solution)/shard_map/ppermute | solution.py:29
  6.1 1.1 fusion.13
  7.2 1.6 %collective-permute-start.3 = (bf16[128,1024]{1,0:T(8,128)(2,1)S(1)}, bf16[128,1024]{1,0:T(8,128)(2,1)}, u32[]{:S(2)}, u32[]{:S(2)}) collective-permute-start(bf16[128,1024]{1,0:T(8,128)(2,1)S(1)} %get-tuple-element.507), channel_id=1, source_target_pairs={{0,1},{1,0},{2,3},{3,2},{4,5},{5,4},{6,7},{7,6},{8,9},{9,8},{10,11... | collective-permute-start | bytes 786440 | tf_op jit(solution)/shard_map/ppermute | solution.py:29
  8.9 1.6 %dynamic-slice_bitcast_fusion.1 = (bf16[64,7392]{1,0:T(8,128)(2,1)S(1)}, bf16[64,7392]{1,0:T(8,128)(2,1)S(1)}) fusion(bf16[2,64,7392]{2,1,0:T(8,128)(2,1)} %param.15, s32[]{:T(128)S(6)} %select_n.206, s32[]{:T(128)S(6)} %select_n.200), kind=kLoop, calls=%fused_computation.31 | loop fusion | bytes 3784712 | tf_op jit(solution)/shard_map/jit(dynamic_index_in_dim)/squeeze | solution.py:317
  10.6 2.7 %dynamic-slice_bitcast_fusion = (bf16[64,7392]{1,0:T(8,128)(2,1)}, bf16[64,7392]{1,0:T(8,128)(2,1)S(1)}) fusion(bf16[2,64,7392]{2,1,0:T(8,128)(2,1)} %param.16, s32[]{:T(128)S(6)} %select_n.206, s32[]{:T(128)S(6)} %select_n.200), kind=kLoop, calls=%fused_computation.30 | loop fusion | bytes 3784712 | tf_op jit(solution)/shard_map/jit(dynamic_index_in_dim)/squeeze | solution.py:317
  14.0 0.9 constant_dynamic-update-slice_fusion.1
  14.9 0.9 constant_dynamic-update-slice_fusion.refs_0_
  16.4 1.8 %collective-permute-done.3 = bf16[128,1024]{1,0:T(8,128)(2,1)} collective-permute-done((bf16[128,1024]{1,0:T(8,128)(2,1)S(1)}, bf16[128,1024]{1,0:T(8,128)(2,1)}, u32[]{:S(2)}, u32[]{:S(2)}) %collective-permute-start.3) | collective-permute-done | bytes 262176 | tf_op jit(solution)/shard_map/ppermute | solution.py:29
  18.2 1.0 broadcast_select_fusion.4
  19.2 1.2 collective-permute-start.7
  20.8 1.6 %collective-permute-start.6 = (bf16[32,7392]{1,0:T(8,128)(2,1)S(1)}, bf16[32,7392]{1,0:T(8,128)(2,1)S(1)}, u32[]{:S(2)}, u32[]{:S(2)}) collective-permute-start(bf16[32,7392]{1,0:T(8,128)(2,1)S(1)} %get-tuple-element.510), channel_id=1, source_target_pairs={{0,16},{4,20},{8,24},{12,28},{16,0},{20,4},{24,8},{28,12},{1,17},{... | collective-permute-start | bytes 1419272 | tf_op jit(solution)/shard_map/ppermute | solution.py:29
  22.4 1.6 %collective-permute-start.5 = (bf16[32,7392]{1,0:T(8,128)(2,1)S(1)}, bf16[32,7392]{1,0:T(8,128)(2,1)S(1)}, u32[]{:S(2)}, u32[]{:S(2)}) collective-permute-start(bf16[32,7392]{1,0:T(8,128)(2,1)S(1)} %get-tuple-element.512), channel_id=1, source_target_pairs={{0,8},{4,12},{8,0},{12,4},{16,24},{20,28},{24,16},{28,20},{1,9},{5... | collective-permute-start | bytes 1419272 | tf_op jit(solution)/shard_map/ppermute | solution.py:29
  24.0 5.8 %collective-permute-done.4.refs_1_ = bf16[192,1024]{1,0:T(8,128)(2,1)S(1)} collective-permute-done((bf16[192,1024]{1,0:T(8,128)(2,1)S(1)}, bf16[192,1024]{1,0:T(8,128)(2,1)S(1)}, u32[]{:S(2)}, u32[]{:S(2)}) %collective-permute-start.4) | collective-permute-done | bytes 393248 | tf_op jit(solution)/shard_map/ppermute | solution.py:29
  29.8 0.6 order_tokens.1.tok
  30.4 1.0 collective-permute-start.10
  31.4 1.6 %collective-permute-done.6 = bf16[32,7392]{1,0:T(8,128)(2,1)S(1)} collective-permute-done((bf16[32,7392]{1,0:T(8,128)(2,1)S(1)}, bf16[32,7392]{1,0:T(8,128)(2,1)S(1)}, u32[]{:S(2)}, u32[]{:S(2)}) %collective-permute-start.6) | collective-permute-done | bytes 473120 | tf_op jit(solution)/shard_map/ppermute | solution.py:29
  33.1 1.6 %collective-permute-start.9 = (bf16[16,7392]{1,0:T(8,128)(2,1)S(1)}, bf16[16,7392]{1,0:T(8,128)(2,1)S(1)}, u32[]{:S(2)}, u32[]{:S(2)}) collective-permute-start(bf16[16,7392]{1,0:T(8,128)(2,1)S(1)} %get-tuple-element.526), channel_id=1, source_target_pairs={{0,8},{4,12},{8,0},{12,4},{16,24},{20,28},{24,16},{28,20},{1,9},{5... | collective-permute-start | bytes 709640 | tf_op jit(solution)/shard_map/ppermute | solution.py:29
  34.8 1.6 %collective-permute-start.8 = (bf16[16,7392]{1,0:T(8,128)(2,1)S(1)}, bf16[16,7392]{1,0:T(8,128)(2,1)S(1)}, u32[]{:S(2)}, u32[]{:S(2)}) collective-permute-start(bf16[16,7392]{1,0:T(8,128)(2,1)S(1)} %get-tuple-element.528), channel_id=1, source_target_pairs={{0,16},{4,20},{8,24},{12,28},{16,0},{20,4},{24,8},{28,12},{1,17},{... | collective-permute-start | bytes 709640 | tf_op jit(solution)/shard_map/ppermute | solution.py:29
  36.4 7.9 %multiply.3 = (bf16[384,2560]{1,0:T(8,128)(2,1)S(1)}, f32[192,2560]{1,0:T(8,128)S(1)}, f32[192,2560]{1,0:T(8,128)S(1)}) custom-call(bf16[384,1024]{1,0:T(8,128)(2,1)S(1)} %order_tokens.1.tok, bf16[7392,1024]{1,0:T(8,128)(2,1)} %bitcast.28, bf16[7392,1024]{1,0:T(8,128)(2,1)} %bitcast.34), custom_call_target="tpu_custom_call" | custom-call | flops 17179869184 | bytes 33554432 | tf_op jit(solution)/shard_map/multiply/pallas_call | solution.py:118
  44.4 0.6 collective-permute-start.13
  45.0 1.3 %collective-permute-start.12 = (bf16[16,7392]{1,0:T(8,128)(2,1)S(1)}, bf16[16,7392]{1,0:T(8,128)(2,1)S(1)}, u32[]{:S(2)}, u32[]{:S(2)}) collective-permute-start(bf16[16,7392]{1,0:T(8,128)(2,1)S(1)} %broadcast_select_fusion.6), channel_id=1, source_target_pairs={{0,16},{4,20},{8,24},{12,28},{16,0},{20,4},{24,8},{28,12},{1,17},{... | collective-permute-start | bytes 709640 | tf_op jit(solution)/shard_map/ppermute | solution.py:29
  46.4 0.8 collective-permute-start.14
  47.2 1.2 collective-permute-done.11
  49.0 0.6 collective-permute-start.15
  49.8 1.3 %collective-permute-start.16 = (bf16[96,2560]{1,0:T(8,128)(2,1)S(1)}, bf16[96,2560]{1,0:T(8,128)(2,1)S(1)}, u32[]{:S(2)}, u32[]{:S(2)}) collective-permute-start(bf16[96,2560]{1,0:T(8,128)(2,1)S(1)} %get-tuple-element.482), channel_id=1, source_target_pairs={{0,16},{4,20},{8,24},{12,28},{16,0},{20,4},{24,8},{28,12},{1,17},{... | collective-permute-start | bytes 1474568 | tf_op jit(solution)/shard_map/ppermute | solution.py:29
  51.1 7.6 %multiply.4 = (bf16[384,2560]{1,0:T(8,128)(2,1)S(1)}, f32[192,2560]{1,0:T(8,128)S(1)}, f32[192,2560]{1,0:T(8,128)S(1)}) custom-call(bf16[384,1024]{1,0:T(8,128)(2,1)S(1)} %order_tokens.1.tok, bf16[7392,1024]{1,0:T(8,128)(2,1)} %bitcast.29, bf16[7392,1024]{1,0:T(8,128)(2,1)} %bitcast.35), custom_call_target="tpu_custom_call" | custom-call | flops 17179869184 | bytes 33554432 | tf_op jit(solution)/shard_map/multiply/pallas_call | solution.py:118
  59.0 0.9 collective-permute-start.19
  59.9 0.6 multiply_lower.1
  60.7 1.6 %collective-permute-start.18 = (bf16[32,7392]{1,0:T(8,128)(2,1)S(1)}, bf16[32,7392]{1,0:T(8,128)(2,1)S(1)}, u32[]{:S(2)}, u32[]{:S(2)}) collective-permute-start(bf16[32,7392]{1,0:T(8,128)(2,1)S(1)} %maximum_select_fusion.4), channel_id=1, source_target_pairs={{0,8},{4,12},{8,0},{12,4},{16,24},{20,28},{24,16},{28,20},{1,9},{5... | collective-permute-start | bytes 1419272 | tf_op jit(solution)/shard_map/ppermute | solution.py:29
  62.2 7.9 %multiply.5 = (bf16[384,2560]{1,0:T(8,128)(2,1)S(1)}, f32[192,2560]{1,0:T(8,128)S(1)}, f32[192,2560]{1,0:T(8,128)S(1)}) custom-call(bf16[384,1024]{1,0:T(8,128)(2,1)S(1)} %order_tokens.1.tok, bf16[7392,1024]{1,0:T(8,128)(2,1)} %bitcast.30, bf16[7392,1024]{1,0:T(8,128)(2,1)} %bitcast.36), custom_call_target="tpu_custom_call" | custom-call | flops 17179869184 | bytes 33554432 | tf_op jit(solution)/shard_map/multiply/pallas_call | solution.py:118
  71.7 2.0 %collective-permute-done.19 = bf16[32,7392]{1,0:T(8,128)(2,1)S(1)} collective-permute-done((bf16[32,7392]{1,0:T(8,128)(2,1)S(1)}, bf16[32,7392]{1,0:T(8,128)(2,1)S(1)}, u32[]{:S(2)}, u32[]{:S(2)}) %collective-permute-start.19) | collective-permute-done | bytes 473120 | tf_op jit(solution)/shard_map/ppermute | solution.py:29
  75.0 1.2 collective-permute-start.23
  76.2 0.8 collective-permute-start.22
  77.0 1.1 collective-permute-done.20.gate_c
  78.4 12.0 %merge.3 = (bf16[7392,1024]{1,0:T(8,128)(2,1)}, bf16[7392,1024]{1,0:T(8,128)(2,1)}) custom-call(bf16[256,1024]{1,0:T(8,128)(2,1)S(1)} %maximum_select_fusion.3.low, bf16[7392,1024]{1,0:T(8,128)(2,1)} %bitcast.31, bf16[7392,1024]{1,0:T(8,128)(2,1)} %bitcast.37, bf16[64,7392]{1,0:T(8,128)(2,1)S(1)} %maximum_select_fusion.gate_b, ...), custom_call_target="tpu_custom_call" | custom-call | flops 1024 | bytes 1024 | tf_op jit(solution)/shard_map/merge/pallas_call | solution.py:188
  90.3 3.1 %collective-permute-done.23.gate_came = bf16[144,2560]{1,0:T(8,128)(2,1)S(1)} collective-permute-done((bf16[144,2560]{1,0:T(8,128)(2,1)S(1)}, bf16[144,2560]{1,0:T(8,128)(2,1)S(1)}, u32[]{:S(2)}, u32[]{:S(2)}) %collective-permute-start.23) | collective-permute-done | bytes 737312 | tf_op jit(solution)/shard_map/ppermute | solution.py:29
  93.4 0.9 collective-permute-done.22.up_came
  95.5 0.9 collective-permute-start.26
  96.8 1.6 %collective-permute-start.25 = (bf16[144,2560]{1,0:T(8,128)(2,1)S(1)}, bf16[144,2560]{1,0:T(8,128)(2,1)S(1)}, u32[]{:S(2)}, u32[]{:S(2)}) collective-permute-start(bf16[144,2560]{1,0:T(8,128)(2,1)S(1)} %pad_maximum_fusion.2), channel_id=1, source_target_pairs={{0,8},{4,12},{8,0},{12,4},{16,24},{20,28},{24,16},{28,20},{1,9},{5... | collective-permute-start | bytes 2211848 | tf_op jit(solution)/shard_map/ppermute | solution.py:29
  98.4 12.0 %merge.4 = (bf16[7392,1024]{1,0:T(8,128)(2,1)}, bf16[7392,1024]{1,0:T(8,128)(2,1)}) custom-call(bf16[256,1024]{1,0:T(8,128)(2,1)S(1)} %maximum_select_fusion.3.low, bf16[7392,1024]{1,0:T(8,128)(2,1)} %bitcast.32, bf16[7392,1024]{1,0:T(8,128)(2,1)} %bitcast.38, ...), custom_call_target="tpu_custom_call", output_to_operand_aliasing={{0}: (7, {}), {1}: (8, {})} | custom-call | flops 1024 | bytes 1024 | tf_op jit(solution)/shard_map/merge/pallas_call | solution.py:188
  110.3 2.6 %collective-permute-done.26.gate_came = bf16[144,2560]{1,0:T(8,128)(2,1)S(1)} collective-permute-done((bf16[144,2560]{1,0:T(8,128)(2,1)S(1)}, bf16[144,2560]{1,0:T(8,128)(2,1)S(1)}, u32[]{:S(2)}, u32[]{:S(2)}) %collective-permute-start.26) | collective-permute-done | bytes 737312 | tf_op jit(solution)/shard_map/ppermute | solution.py:29
  112.9 1.0 collective-permute-done.25.up_came
  114.1 1.6 %collective-permute-start.27 = (bf16[48,2560]{1,0:T(8,128)(2,1)S(1)}, bf16[48,2560]{1,0:T(8,128)(2,1)S(1)}, u32[]{:S(2)}, u32[]{:S(2)}) collective-permute-start(bf16[48,2560]{1,0:T(8,128)(2,1)S(1)} %get-tuple-element.486), channel_id=1, source_target_pairs={{0,8},{4,12},{8,0},{12,4},{16,24},{20,28},{24,16},{28,20},{1,9},{5... | collective-permute-start | bytes 737288 | tf_op jit(solution)/shard_map/ppermute | solution.py:29
  115.9 0.7 collective-permute-start.28
  116.5 5.8 %merge.5 = (bf16[7392,1024]{1,0:T(8,128)(2,1)}, bf16[7392,1024]{1,0:T(8,128)(2,1)}) custom-call(bf16[256,1024]{1,0:T(8,128)(2,1)S(1)} %maximum_select_fusion.3.low, bf16[7392,1024]{1,0:T(8,128)(2,1)} %bitcast.33, bf16[7392,1024]{1,0:T(8,128)(2,1)} %bitcast.39, ...), custom_call_target="tpu_custom_call", output_to_operand_aliasing={{0}: (7, {}), {1}: (8, {})} | custom-call | flops 1024 | bytes 1024 | tf_op jit(solution)/shard_map/merge/pallas_call | solution.py:188
  122.7 1.2 finish.3.refs_0_
  123.9 1.2 finish.4.refs_0_
  125.1 1.2 finish.5
  (85 shorter events, 8.5 us)
Async XLA Ops:
  0.6 14.3 %collective-permute-start = (bf16[96,1024]{1,0:T(8,128)(2,1)}, bf16[96,1024]{1,0:T(8,128)(2,1)}, u32[]{:S(2)}, u32[]{:S(2)}) collective-permute-start(bf16[96,1024]{1,0:T(8,128)(2,1)} %param.10), channel_id=1, source_target_pairs={{0,2},{1,3},{2,0},{3,1},{4,6},{5,7},{6,4},{7,5},{8,10},{9,11},{10,... | collective-permute-start | bytes 589832 | tf_op jit(solution)/shard_map/ppermute | solution.py:29
  7.2 11.0 %collective-permute-start.3 = (bf16[128,1024]{1,0:T(8,128)(2,1)S(1)}, bf16[128,1024]{1,0:T(8,128)(2,1)}, u32[]{:S(2)}, u32[]{:S(2)}) collective-permute-start(bf16[128,1024]{1,0:T(8,128)(2,1)S(1)} %get-tuple-element.507), channel_id=1, source_target_pairs={{0,1},{1,0},{2,3},{3,2},{4,5},{5,4},{6,7},{7,6},{8,9},{9,8},{10,11... | collective-permute-start | bytes 786440 | tf_op jit(solution)/shard_map/ppermute | solution.py:29
  10.5 3.3 %copy-start = (s32[4]{0:T(128)S(1)}, s32[4]{0:T(128)}, u32[]{:S(2)}) copy-start(s32[4]{0:T(128)} %constant.91.clone) | copy-start | bytes 52
  10.5 10.0 %collective-permute-start.1 = (bf16[64,7392]{1,0:T(8,128)(2,1)S(1)}, bf16[64,7392]{1,0:T(8,128)(2,1)}, u32[]{:S(2)}, u32[]{:S(2)}) collective-permute-start(bf16[64,7392]{1,0:T(8,128)(2,1)S(1)} %get-tuple-element.505), channel_id=1, source_target_pairs={{0,4},{4,0},{8,12},{12,8},{16,20},{20,16},{24,28},{28,24},{1,5},{5... | collective-permute-start | bytes 2838536 | tf_op jit(solution)/shard_map/ppermute | solution.py:29
  13.3 7.2 %collective-permute-start.2 = (bf16[64,7392]{1,0:T(8,128)(2,1)}, bf16[64,7392]{1,0:T(8,128)(2,1)}, u32[]{:S(2)}, u32[]{:S(2)}) collective-permute-start(bf16[64,7392]{1,0:T(8,128)(2,1)} %get-tuple-element.503), channel_id=1, source_target_pairs={{0,4},{4,0},{8,12},{12,8},{16,20},{20,16},{24,28},{28,24},{1,5},{5... | collective-permute-start | bytes 2838536 | tf_op jit(solution)/shard_map/ppermute | solution.py:29
  15.9 13.9 %collective-permute-start.4 = (bf16[192,1024]{1,0:T(8,128)(2,1)S(1)}, bf16[192,1024]{1,0:T(8,128)(2,1)S(1)}, u32[]{:S(2)}, u32[]{:S(2)}) collective-permute-start(bf16[192,1024]{1,0:T(8,128)(2,1)S(1)} %constant_dynamic-update-slice_fusion.refs_0_), channel_id=1, source_target_pairs={{0,1},{1,0},{2,3},{3,2},{4,5},{5,4},{6,7},{7,6},{8,9},{9,8},{10,11... | collective-permute-start | bytes 1179656 | tf_op jit(solution)/shard_map/ppermute | solution.py:29
  19.2 11.2 %collective-permute-start.7 = (bf16[64,1024]{1,0:T(8,128)(2,1)S(1)}, bf16[64,1024]{1,0:T(8,128)(2,1)S(1)}, u32[]{:S(2)}, u32[]{:S(2)}) collective-permute-start(bf16[64,1024]{1,0:T(8,128)(2,1)S(1)} %get-tuple-element.530), channel_id=1, source_target_pairs={{0,2},{1,3},{2,0},{3,1},{4,6},{5,7},{6,4},{7,5},{8,10},{9,11},{10,... | collective-permute-start | bytes 393224 | tf_op jit(solution)/shard_map/ppermute | solution.py:29
  20.8 12.2 %collective-permute-start.6 = (bf16[32,7392]{1,0:T(8,128)(2,1)S(1)}, bf16[32,7392]{1,0:T(8,128)(2,1)S(1)}, u32[]{:S(2)}, u32[]{:S(2)}) collective-permute-start(bf16[32,7392]{1,0:T(8,128)(2,1)S(1)} %get-tuple-element.510), channel_id=1, source_target_pairs={{0,16},{4,20},{8,24},{12,28},{16,0},{20,4},{24,8},{28,12},{1,17},{... | collective-permute-start | bytes 1419272 | tf_op jit(solution)/shard_map/ppermute | solution.py:29
  22.4 12.3 %collective-permute-start.5 = (bf16[32,7392]{1,0:T(8,128)(2,1)S(1)}, bf16[32,7392]{1,0:T(8,128)(2,1)S(1)}, u32[]{:S(2)}, u32[]{:S(2)}) collective-permute-start(bf16[32,7392]{1,0:T(8,128)(2,1)S(1)} %get-tuple-element.512), channel_id=1, source_target_pairs={{0,8},{4,12},{8,0},{12,4},{16,24},{20,28},{24,16},{28,20},{1,9},{5... | collective-permute-start | bytes 1419272 | tf_op jit(solution)/shard_map/ppermute | solution.py:29
  30.4 13.9 %collective-permute-start.10 = (bf16[64,1024]{1,0:T(8,128)(2,1)S(1)}, bf16[64,1024]{1,0:T(8,128)(2,1)S(1)}, u32[]{:S(2)}, u32[]{:S(2)}) collective-permute-start(bf16[64,1024]{1,0:T(8,128)(2,1)S(1)} %broadcast_select_fusion.7), channel_id=1, source_target_pairs={{0,2},{1,3},{2,0},{3,1},{4,6},{5,7},{6,4},{7,5},{8,10},{9,11},{10,... | collective-permute-start | bytes 393224 | tf_op jit(solution)/shard_map/ppermute | solution.py:29
  33.1 11.2 %collective-permute-start.9 = (bf16[16,7392]{1,0:T(8,128)(2,1)S(1)}, bf16[16,7392]{1,0:T(8,128)(2,1)S(1)}, u32[]{:S(2)}, u32[]{:S(2)}) collective-permute-start(bf16[16,7392]{1,0:T(8,128)(2,1)S(1)} %get-tuple-element.526), channel_id=1, source_target_pairs={{0,8},{4,12},{8,0},{12,4},{16,24},{20,28},{24,16},{28,20},{1,9},{5... | collective-permute-start | bytes 709640 | tf_op jit(solution)/shard_map/ppermute | solution.py:29
  34.8 9.5 %collective-permute-start.8 = (bf16[16,7392]{1,0:T(8,128)(2,1)S(1)}, bf16[16,7392]{1,0:T(8,128)(2,1)S(1)}, u32[]{:S(2)}, u32[]{:S(2)}) collective-permute-start(bf16[16,7392]{1,0:T(8,128)(2,1)S(1)} %get-tuple-element.528), channel_id=1, source_target_pairs={{0,16},{4,20},{8,24},{12,28},{16,0},{20,4},{24,8},{28,12},{1,17},{... | collective-permute-start | bytes 709640 | tf_op jit(solution)/shard_map/ppermute | solution.py:29
  44.3 4.0 %collective-permute-start.11 = (bf16[384,2560]{1,0:T(8,128)(2,1)S(1)}, bf16[384,2560]{1,0:T(8,128)(2,1)S(1)}, u32[]{:S(2)}, u32[]{:S(2)}) collective-permute-start(bf16[384,2560]{1,0:T(8,128)(2,1)S(1)} %get-tuple-element.265), channel_id=1, source_target_pairs={{0,4},{4,0},{8,12},{12,8},{16,20},{20,16},{24,28},{28,24},{1,5},{5... | collective-permute-start | bytes 5898248 | tf_op jit(solution)/shard_map/ppermute | solution.py:29
  44.4 14.3 %collective-permute-start.13 = (bf16[16,7392]{1,0:T(8,128)(2,1)S(1)}, bf16[16,7392]{1,0:T(8,128)(2,1)S(1)}, u32[]{:S(2)}, u32[]{:S(2)}) collective-permute-start(bf16[16,7392]{1,0:T(8,128)(2,1)S(1)} %broadcast_select_fusion.5), channel_id=1, source_target_pairs={{0,8},{4,12},{8,0},{12,4},{16,24},{20,28},{24,16},{28,20},{1,9},{5... | collective-permute-start | bytes 709640 | tf_op jit(solution)/shard_map/ppermute | solution.py:29
  45.0 13.7 %collective-permute-start.12 = (bf16[16,7392]{1,0:T(8,128)(2,1)S(1)}, bf16[16,7392]{1,0:T(8,128)(2,1)S(1)}, u32[]{:S(2)}, u32[]{:S(2)}) collective-permute-start(bf16[16,7392]{1,0:T(8,128)(2,1)S(1)} %broadcast_select_fusion.6), channel_id=1, source_target_pairs={{0,16},{4,20},{8,24},{12,28},{16,0},{20,4},{24,8},{28,12},{1,17},{... | collective-permute-start | bytes 709640 | tf_op jit(solution)/shard_map/ppermute | solution.py:29
  46.4 12.3 %collective-permute-start.14 = (bf16[128,1024]{1,0:T(8,128)(2,1)S(1)}, bf16[128,1024]{1,0:T(8,128)(2,1)S(1)}, u32[]{:S(2)}, u32[]{:S(2)}) collective-permute-start(bf16[128,1024]{1,0:T(8,128)(2,1)S(1)} %maximum_select_fusion.6), channel_id=1, source_target_pairs={{0,1},{1,0},{2,3},{3,2},{4,5},{5,4},{6,7},{7,6},{8,9},{9,8},{10,11... | collective-permute-start | bytes 786440 | tf_op jit(solution)/shard_map/ppermute | solution.py:29
  49.0 21.1 %collective-permute-start.15 = (bf16[96,2560]{1,0:T(8,128)(2,1)S(1)}, bf16[96,2560]{1,0:T(8,128)(2,1)S(1)}, u32[]{:S(2)}, u32[]{:S(2)}) collective-permute-start(bf16[96,2560]{1,0:T(8,128)(2,1)S(1)} %get-tuple-element.484), channel_id=1, source_target_pairs={{0,8},{4,12},{8,0},{12,4},{16,24},{20,28},{24,16},{28,20},{1,9},{5... | collective-permute-start | bytes 1474568 | tf_op jit(solution)/shard_map/ppermute | solution.py:29
  49.8 20.6 %collective-permute-start.16 = (bf16[96,2560]{1,0:T(8,128)(2,1)S(1)}, bf16[96,2560]{1,0:T(8,128)(2,1)S(1)}, u32[]{:S(2)}, u32[]{:S(2)}) collective-permute-start(bf16[96,2560]{1,0:T(8,128)(2,1)S(1)} %get-tuple-element.482), channel_id=1, source_target_pairs={{0,16},{4,20},{8,24},{12,28},{16,0},{20,4},{24,8},{28,12},{1,17},{... | collective-permute-start | bytes 1474568 | tf_op jit(solution)/shard_map/ppermute | solution.py:29
  59.0 14.7 %collective-permute-start.19 = (bf16[32,7392]{1,0:T(8,128)(2,1)S(1)}, bf16[32,7392]{1,0:T(8,128)(2,1)S(1)}, u32[]{:S(2)}, u32[]{:S(2)}) collective-permute-start(bf16[32,7392]{1,0:T(8,128)(2,1)S(1)} %maximum_select_fusion.5), channel_id=1, source_target_pairs={{0,16},{4,20},{8,24},{12,28},{16,0},{20,4},{24,8},{28,12},{1,17},{... | collective-permute-start | bytes 1419272 | tf_op jit(solution)/shard_map/ppermute | solution.py:29
  60.5 9.9 %collective-permute-start.17 = (bf16[384,2560]{1,0:T(8,128)(2,1)S(1)}, bf16[384,2560]{1,0:T(8,128)(2,1)S(1)}, u32[]{:S(2)}, u32[]{:S(2)}) collective-permute-start(bf16[384,2560]{1,0:T(8,128)(2,1)S(1)} %get-tuple-element.324), channel_id=1, source_target_pairs={{0,4},{4,0},{8,12},{12,8},{16,20},{20,16},{24,28},{28,24},{1,5},{5... | collective-permute-start | bytes 5898248 | tf_op jit(solution)/shard_map/ppermute | solution.py:29
  60.7 13.3 %collective-permute-start.18 = (bf16[32,7392]{1,0:T(8,128)(2,1)S(1)}, bf16[32,7392]{1,0:T(8,128)(2,1)S(1)}, u32[]{:S(2)}, u32[]{:S(2)}) collective-permute-start(bf16[32,7392]{1,0:T(8,128)(2,1)S(1)} %maximum_select_fusion.4), channel_id=1, source_target_pairs={{0,8},{4,12},{8,0},{12,4},{16,24},{20,28},{24,16},{28,20},{1,9},{5... | collective-permute-start | bytes 1419272 | tf_op jit(solution)/shard_map/ppermute | solution.py:29
  70.2 20.2 %collective-permute-start.24 = (bf16[384,2560]{1,0:T(8,128)(2,1)S(1)}, bf16[384,2560]{1,0:T(8,128)(2,1)S(1)}, u32[]{:S(2)}, u32[]{:S(2)}) collective-permute-start(bf16[384,2560]{1,0:T(8,128)(2,1)S(1)} %get-tuple-element.381), channel_id=1, source_target_pairs={{0,4},{4,0},{8,12},{12,8},{16,20},{20,16},{24,28},{28,24},{1,5},{5... | collective-permute-start | bytes 5898248 | tf_op jit(solution)/shard_map/ppermute | solution.py:29
  74.2 2.8 %collective-permute-start.21 = (bf16[64,7392]{1,0:T(8,128)(2,1)S(1)}, bf16[64,7392]{1,0:T(8,128)(2,1)S(1)}, u32[]{:S(2)}, u32[]{:S(2)}) collective-permute-start(bf16[64,7392]{1,0:T(8,128)(2,1)S(1)} %maximum_select_fusion.1.up_b), channel_id=1, source_target_pairs={{0,4},{4,0},{8,12},{12,8},{16,20},{20,16},{24,28},{28,24},{1,5},{5... | collective-permute-start | bytes 2838536 | tf_op jit(solution)/shard_map/ppermute | solution.py:29
  74.4 3.7 %collective-permute-start.20 = (bf16[64,7392]{1,0:T(8,128)(2,1)S(1)}, bf16[64,7392]{1,0:T(8,128)(2,1)S(1)}, u32[]{:S(2)}, u32[]{:S(2)}) collective-permute-start(bf16[64,7392]{1,0:T(8,128)(2,1)S(1)} %maximum_select_fusion.gate_b), channel_id=1, source_target_pairs={{0,4},{4,0},{8,12},{12,8},{16,20},{20,16},{24,28},{28,24},{1,5},{5... | collective-permute-start | bytes 2838536 | tf_op jit(solution)/shard_map/ppermute | solution.py:29
  75.0 18.5 %collective-permute-start.23 = (bf16[144,2560]{1,0:T(8,128)(2,1)S(1)}, bf16[144,2560]{1,0:T(8,128)(2,1)S(1)}, u32[]{:S(2)}, u32[]{:S(2)}) collective-permute-start(bf16[144,2560]{1,0:T(8,128)(2,1)S(1)} %pad_maximum_fusion.1), channel_id=1, source_target_pairs={{0,16},{4,20},{8,24},{12,28},{16,0},{20,4},{24,8},{28,12},{1,17},{... | collective-permute-start | bytes 2211848 | tf_op jit(solution)/shard_map/ppermute | solution.py:29
  76.2 18.2 %collective-permute-start.22 = (bf16[144,2560]{1,0:T(8,128)(2,1)S(1)}, bf16[144,2560]{1,0:T(8,128)(2,1)S(1)}, u32[]{:S(2)}, u32[]{:S(2)}) collective-permute-start(bf16[144,2560]{1,0:T(8,128)(2,1)S(1)} %pad_maximum_fusion), channel_id=1, source_target_pairs={{0,8},{4,12},{8,0},{12,4},{16,24},{20,28},{24,16},{28,20},{1,9},{5... | collective-permute-start | bytes 2211848 | tf_op jit(solution)/shard_map/ppermute | solution.py:29
  95.5 17.4 %collective-permute-start.26 = (bf16[144,2560]{1,0:T(8,128)(2,1)S(1)}, bf16[144,2560]{1,0:T(8,128)(2,1)S(1)}, u32[]{:S(2)}, u32[]{:S(2)}) collective-permute-start(bf16[144,2560]{1,0:T(8,128)(2,1)S(1)} %pad_maximum_fusion.3), channel_id=1, source_target_pairs={{0,16},{4,20},{8,24},{12,28},{16,0},{20,4},{24,8},{28,12},{1,17},{... | collective-permute-start | bytes 2211848 | tf_op jit(solution)/shard_map/ppermute | solution.py:29
  96.8 17.1 %collective-permute-start.25 = (bf16[144,2560]{1,0:T(8,128)(2,1)S(1)}, bf16[144,2560]{1,0:T(8,128)(2,1)S(1)}, u32[]{:S(2)}, u32[]{:S(2)}) collective-permute-start(bf16[144,2560]{1,0:T(8,128)(2,1)S(1)} %pad_maximum_fusion.2), channel_id=1, source_target_pairs={{0,8},{4,12},{8,0},{12,4},{16,24},{20,28},{24,16},{28,20},{1,9},{5... | collective-permute-start | bytes 2211848 | tf_op jit(solution)/shard_map/ppermute | solution.py:29
  114.1 8.2 %collective-permute-start.27 = (bf16[48,2560]{1,0:T(8,128)(2,1)S(1)}, bf16[48,2560]{1,0:T(8,128)(2,1)S(1)}, u32[]{:S(2)}, u32[]{:S(2)}) collective-permute-start(bf16[48,2560]{1,0:T(8,128)(2,1)S(1)} %get-tuple-element.486), channel_id=1, source_target_pairs={{0,8},{4,12},{8,0},{12,4},{16,24},{20,28},{24,16},{28,20},{1,9},{5... | collective-permute-start | bytes 737288 | tf_op jit(solution)/shard_map/ppermute | solution.py:29
  115.9 6.5 %collective-permute-start.28 = (bf16[48,2560]{1,0:T(8,128)(2,1)S(1)}, bf16[48,2560]{1,0:T(8,128)(2,1)S(1)}, u32[]{:S(2)}, u32[]{:S(2)}) collective-permute-start(bf16[48,2560]{1,0:T(8,128)(2,1)S(1)} %get-tuple-element.488), channel_id=1, source_target_pairs={{0,16},{4,20},{8,24},{12,28},{16,0},{20,4},{24,8},{28,12},{1,17},{... | collective-permute-start | bytes 737288 | tf_op jit(solution)/shard_map/ppermute | solution.py:29

commit v2 on v1

--- a/solution.py
+++ b/solution.py
@@ -418,25 +418,31 @@
     state["uppers"] = [part for f in uppers for part in (f.held, f.arrived[0])]
     state["low"] = by_core(state["low"], 0)
     fence()
-    cuts = [0, used * 2 // 5, used * 4 // 5, used]
+    small = pl.cdiv(used, 16)
+    cuts = [0, (used - small + 1) // 2, used - small, used]
+    def finish(chosen, hidden):
+        if chosen and "correction" not in state:
+            ends = sums[turns[min(1, len(turns) - 1)]].finish()
+            correction = jnp.concatenate([end[:, columns - 2 * rank :] for end in ends], axis=1)
+            state["correction"] = by_core(correction, 1)
+        for turn in chosen:
+            hidden = finished(turn, sums[turn], state["correction"], state["uppers"], units, hidden)
+        return hidden
+
     state["merged"] = []
-    done = 0
     for first, last in zip(cuts, cuts[1:]):
         state["merged"] = merge_span(
             (first, last - first), weights, state["low"], state["uppers"], state["merged"]
         )
+        if last == used:
+            early = [t for t in turns[:-1] if all(sums[i].step == stages for i in turns[:-1])]
+            state["hidden"] = finish(early, [])
         fence(*flying, *[sums[turn] for turn in turns[2:] if sums[turn].step == 0])
         flying = step()
         fence()
     while flying:
         flying = step()
-
-    ends = sums[turns[min(1, len(turns) - 1)]].finish()
-    correction = jnp.concatenate([end[:, columns - 2 * rank :] for end in ends], axis=1)
-    correction = by_core(correction, 1)
-    hidden = []
-    for turn in turns:
-        hidden = finished(turn, sums[turn], correction, state["uppers"], units, hidden)
+    hidden = finish([turn for turn in turns if turn not in early], state["hidden"])
     merged = state["merged"]
     return merged[0].T, merged[1].T, hidden[0]
 

time: 128 us -> 125 us (0.977); the launches traced: 126 us -> 125 us
  waiting for transfers between devices: 21.5 us -> 17.4 us
  Pallas kernels: 57.9 us -> 61 us
    ppermute x29, waiting for transfers between devices: 21.5 us -> 17.4 us  [swap(): return lax.ppermute(value, axis, [(i, i ^ distance) for i in range(size)])]
    pallas_call x3, Pallas kernels: 29.8 us -> 32.8 us  [merge_span(): pl.pallas_call(merge_kernel, grid=(count,), out_shape=[jax.ShapeDtypeStru...]
  transfers between devices with their start and end apart: 29 -> 29, of which waited for: 11 -> 10; matrix products, arithmetic and copies ran while one was open for 10% -> 10% of each run, Pallas kernels for 43% -> 48%
where the time goes in v2:
time: 125 us
  Pallas kernels  61 us (49%)
  starting transfers between devices  30.4 us (24%)
  waiting for transfers between devices  17.4 us (14%)
  other arithmetic  6.71 us (5%)
  local copies, waits for them, and re-layouts  6.55 us (5%)
  between operations  2.51 us (2%)
    pallas_call x3, Pallas kernels, merge_span(): pl.pallas_call(merge_kernel, grid=(count,), out_shape=[jax.ShapeDtypeStru...  32.8 us
    ppermute x29, starting transfers between devices, swap(): return lax.ppermute(value, axis, [(i, i ^ distance) for i in range(size)])  30.4 us
    pallas_call x3, Pallas kernels, multiply_chunk(): pl.pallas_call(functools.partial(multiply_kernel, rows, places), grid=(co...  23.4 us
    ppermute x29, waiting for transfers between devices, swap(): return lax.ppermute(value, axis, [(i, i ^ distance) for i in range(size)])  17.4 us
    squeeze x2, local copies, waits for them, and re-layouts, slot(): return lax.dynamic_index_in_dim(stack, i, 0, keepdims=False)  4.14 us
    pallas_call x3, Pallas kernels, finished(): pl.pallas_call(finish_kernel, grid=(1,), out_shape=[jax.ShapeDtypeStruct(...  3.56 us
  transfers between devices with their start and end apart: 29, of which 10 were waited for; matrix products, arithmetic and copies ran while one was open for 10% of the time, Pallas kernels for 48%

profile of v2, /device:TPU:0, one launch (start us, length us, event | category | flops | bytes accessed | tf_op | source)
XLA Modules:
  0.0 124.6 jit_solution(935516863117589688)
XLA Ops:
  0.6 4.1 %collective-permute-start = (bf16[96,1024]{1,0:T(8,128)(2,1)}, bf16[96,1024]{1,0:T(8,128)(2,1)}, u32[]{:S(2)}, u32[]{:S(2)}) collective-permute-start(bf16[96,1024]{1,0:T(8,128)(2,1)} %param.10), channel_id=1, source_target_pairs={{0,2},{1,3},{2,0},{3,1},{4,6},{5,7},{6,4},{7,5},{8,10},{9,11},{10,... | collective-permute-start | bytes 589832 | tf_op jit(solution)/shard_map/ppermute | solution.py:29
  6.1 1.1 fusion.13
  7.2 1.6 %collective-permute-start.3 = (bf16[128,1024]{1,0:T(8,128)(2,1)S(1)}, bf16[128,1024]{1,0:T(8,128)(2,1)}, u32[]{:S(2)}, u32[]{:S(2)}) collective-permute-start(bf16[128,1024]{1,0:T(8,128)(2,1)S(1)} %get-tuple-element.499), channel_id=1, source_target_pairs={{0,1},{1,0},{2,3},{3,2},{4,5},{5,4},{6,7},{7,6},{8,9},{9,8},{10,11... | collective-permute-start | bytes 786440 | tf_op jit(solution)/shard_map/ppermute | solution.py:29
  8.9 1.6 %dynamic-slice_bitcast_fusion.1 = (bf16[64,7392]{1,0:T(8,128)(2,1)S(1)}, bf16[64,7392]{1,0:T(8,128)(2,1)S(1)}) fusion(bf16[2,64,7392]{2,1,0:T(8,128)(2,1)} %param.15, s32[]{:T(128)S(6)} %select_n.207, s32[]{:T(128)S(6)} %select_n.201), kind=kLoop, calls=%fused_computation.31 | loop fusion | bytes 3784712 | tf_op jit(solution)/shard_map/jit(dynamic_index_in_dim)/squeeze | solution.py:317
  10.6 2.5 %dynamic-slice_bitcast_fusion = (bf16[64,7392]{1,0:T(8,128)(2,1)}, bf16[64,7392]{1,0:T(8,128)(2,1)S(1)}) fusion(bf16[2,64,7392]{2,1,0:T(8,128)(2,1)} %param.16, s32[]{:T(128)S(6)} %select_n.207, s32[]{:T(128)S(6)} %select_n.201), kind=kLoop, calls=%fused_computation.30 | loop fusion | bytes 3784712 | tf_op jit(solution)/shard_map/jit(dynamic_index_in_dim)/squeeze | solution.py:317
  13.1 0.5 collective-permute-start.2
  13.8 0.9 constant_dynamic-update-slice_fusion.1
  14.7 0.9 constant_dynamic-update-slice_fusion.refs_0_
  15.7 0.5 collective-permute-start.4
  16.2 2.0 %collective-permute-done.3 = bf16[128,1024]{1,0:T(8,128)(2,1)} collective-permute-done((bf16[128,1024]{1,0:T(8,128)(2,1)S(1)}, bf16[128,1024]{1,0:T(8,128)(2,1)}, u32[]{:S(2)}, u32[]{:S(2)}) %collective-permute-start.3) | collective-permute-done | bytes 262176 | tf_op jit(solution)/shard_map/ppermute | solution.py:29
  18.3 1.2 collective-permute-start.7
  19.8 1.6 %collective-permute-start.6 = (bf16[32,7392]{1,0:T(8,128)(2,1)S(1)}, bf16[32,7392]{1,0:T(8,128)(2,1)S(1)}, u32[]{:S(2)}, u32[]{:S(2)}) collective-permute-start(bf16[32,7392]{1,0:T(8,128)(2,1)S(1)} %get-tuple-element.502), channel_id=1, source_target_pairs={{0,16},{4,20},{8,24},{12,28},{16,0},{20,4},{24,8},{28,12},{1,17},{... | collective-permute-start | bytes 1419272 | tf_op jit(solution)/shard_map/ppermute | solution.py:29
  21.5 1.6 %collective-permute-start.5 = (bf16[32,7392]{1,0:T(8,128)(2,1)S(1)}, bf16[32,7392]{1,0:T(8,128)(2,1)S(1)}, u32[]{:S(2)}, u32[]{:S(2)}) collective-permute-start(bf16[32,7392]{1,0:T(8,128)(2,1)S(1)} %get-tuple-element.504), channel_id=1, source_target_pairs={{0,8},{4,12},{8,0},{12,4},{16,24},{20,28},{24,16},{28,20},{1,9},{5... | collective-permute-start | bytes 1419272 | tf_op jit(solution)/shard_map/ppermute | solution.py:29
  23.0 6.6 %collective-permute-done.4.refs_1_ = bf16[192,1024]{1,0:T(8,128)(2,1)S(1)} collective-permute-done((bf16[192,1024]{1,0:T(8,128)(2,1)S(1)}, bf16[192,1024]{1,0:T(8,128)(2,1)S(1)}, u32[]{:S(2)}, u32[]{:S(2)}) %collective-permute-start.4) | collective-permute-done | bytes 393248 | tf_op jit(solution)/shard_map/ppermute | solution.py:29
  29.6 0.6 order_tokens.1.tok
  30.2 1.1 collective-permute-start.10
  31.4 2.1 %collective-permute-done.6 = bf16[32,7392]{1,0:T(8,128)(2,1)S(1)} collective-permute-done((bf16[32,7392]{1,0:T(8,128)(2,1)S(1)}, bf16[32,7392]{1,0:T(8,128)(2,1)S(1)}, u32[]{:S(2)}, u32[]{:S(2)}) %collective-permute-start.6) | collective-permute-done | bytes 473120 | tf_op jit(solution)/shard_map/ppermute | solution.py:29
  33.6 1.6 %collective-permute-start.9 = (bf16[16,7392]{1,0:T(8,128)(2,1)S(1)}, bf16[16,7392]{1,0:T(8,128)(2,1)S(1)}, u32[]{:S(2)}, u32[]{:S(2)}) collective-permute-start(bf16[16,7392]{1,0:T(8,128)(2,1)S(1)} %get-tuple-element.518), channel_id=1, source_target_pairs={{0,8},{4,12},{8,0},{12,4},{16,24},{20,28},{24,16},{28,20},{1,9},{5... | collective-permute-start | bytes 709640 | tf_op jit(solution)/shard_map/ppermute | solution.py:29
  35.3 1.6 %collective-permute-start.8 = (bf16[16,7392]{1,0:T(8,128)(2,1)S(1)}, bf16[16,7392]{1,0:T(8,128)(2,1)S(1)}, u32[]{:S(2)}, u32[]{:S(2)}) collective-permute-start(bf16[16,7392]{1,0:T(8,128)(2,1)S(1)} %get-tuple-element.520), channel_id=1, source_target_pairs={{0,16},{4,20},{8,24},{12,28},{16,0},{20,4},{24,8},{28,12},{1,17},{... | collective-permute-start | bytes 709640 | tf_op jit(solution)/shard_map/ppermute | solution.py:29
  36.9 7.9 %multiply.3 = (bf16[384,2560]{1,0:T(8,128)(2,1)S(1)}, f32[192,2560]{1,0:T(8,128)S(1)}, f32[192,2560]{1,0:T(8,128)S(1)}) custom-call(bf16[384,1024]{1,0:T(8,128)(2,1)S(1)} %order_tokens.1.tok, bf16[7392,1024]{1,0:T(8,128)(2,1)} %bitcast.28, bf16[7392,1024]{1,0:T(8,128)(2,1)} %bitcast.34), custom_call_target="tpu_custom_call" | custom-call | flops 17179869184 | bytes 33554432 | tf_op jit(solution)/shard_map/multiply/pallas_call | solution.py:118
  44.9 0.6 collective-permute-start.13
  45.6 1.2 collective-permute-start.12
  46.9 0.8 collective-permute-start.14
  47.7 1.2 collective-permute-done.11
  49.6 0.6 collective-permute-start.15
  50.4 1.2 collective-permute-start.16
  51.6 7.6 %multiply.4 = (bf16[384,2560]{1,0:T(8,128)(2,1)S(1)}, f32[192,2560]{1,0:T(8,128)S(1)}, f32[192,2560]{1,0:T(8,128)S(1)}) custom-call(bf16[384,1024]{1,0:T(8,128)(2,1)S(1)} %order_tokens.1.tok, bf16[7392,1024]{1,0:T(8,128)(2,1)} %bitcast.29, bf16[7392,1024]{1,0:T(8,128)(2,1)} %bitcast.35), custom_call_target="tpu_custom_call" | custom-call | flops 17179869184 | bytes 33554432 | tf_op jit(solution)/shard_map/multiply/pallas_call | solution.py:118
  59.5 0.9 collective-permute-start.19
  60.4 0.6 multiply_lower.1
  61.2 1.6 %collective-permute-start.18 = (bf16[32,7392]{1,0:T(8,128)(2,1)S(1)}, bf16[32,7392]{1,0:T(8,128)(2,1)S(1)}, u32[]{:S(2)}, u32[]{:S(2)}) collective-permute-start(bf16[32,7392]{1,0:T(8,128)(2,1)S(1)} %maximum_select_fusion.4), channel_id=1, source_target_pairs={{0,8},{4,12},{8,0},{12,4},{16,24},{20,28},{24,16},{28,20},{1,9},{5... | collective-permute-start | bytes 1419272 | tf_op jit(solution)/shard_map/ppermute | solution.py:29
  62.8 7.9 %multiply.5 = (bf16[384,2560]{1,0:T(8,128)(2,1)S(1)}, f32[192,2560]{1,0:T(8,128)S(1)}, f32[192,2560]{1,0:T(8,128)S(1)}) custom-call(bf16[384,1024]{1,0:T(8,128)(2,1)S(1)} %order_tokens.1.tok, bf16[7392,1024]{1,0:T(8,128)(2,1)} %bitcast.30, bf16[7392,1024]{1,0:T(8,128)(2,1)} %bitcast.36), custom_call_target="tpu_custom_call" | custom-call | flops 17179869184 | bytes 33554432 | tf_op jit(solution)/shard_map/multiply/pallas_call | solution.py:118
  72.3 2.0 %collective-permute-done.19 = bf16[32,7392]{1,0:T(8,128)(2,1)S(1)} collective-permute-done((bf16[32,7392]{1,0:T(8,128)(2,1)S(1)}, bf16[32,7392]{1,0:T(8,128)(2,1)S(1)}, u32[]{:S(2)}, u32[]{:S(2)}) %collective-permute-start.19) | collective-permute-done | bytes 473120 | tf_op jit(solution)/shard_map/ppermute | solution.py:29
  74.9 0.6 collective-permute-start.20
  75.5 1.2 collective-permute-start.23
  76.7 0.8 collective-permute-start.22
  77.5 1.1 collective-permute-done.20.gate_c
  78.9 15.0 %merge.3 = (bf16[7392,1024]{1,0:T(8,128)(2,1)}, bf16[7392,1024]{1,0:T(8,128)(2,1)}) custom-call(bf16[256,1024]{1,0:T(8,128)(2,1)S(1)} %maximum_select_fusion.3.low, bf16[7392,1024]{1,0:T(8,128)(2,1)} %bitcast.31, bf16[7392,1024]{1,0:T(8,128)(2,1)} %bitcast.37, bf16[64,7392]{1,0:T(8,128)(2,1)S(1)} %maximum_select_fusion.gate_b, ...), custom_call_target="tpu_custom_call" | custom-call | flops 1024 | bytes 1024 | tf_op jit(solution)/shard_map/merge/pallas_call | solution.py:188
  94.0 0.9 collective-permute-done.22.up_came
  96.0 0.9 collective-permute-start.26
  97.3 1.6 %collective-permute-start.25 = (bf16[144,2560]{1,0:T(8,128)(2,1)S(1)}, bf16[144,2560]{1,0:T(8,128)(2,1)S(1)}, u32[]{:S(2)}, u32[]{:S(2)}) collective-permute-start(bf16[144,2560]{1,0:T(8,128)(2,1)S(1)} %pad_maximum_fusion.2), channel_id=1, source_target_pairs={{0,8},{4,12},{8,0},{12,4},{16,24},{20,28},{24,16},{28,20},{1,9},{5... | collective-permute-start | bytes 2211848 | tf_op jit(solution)/shard_map/ppermute | solution.py:29
  98.9 15.0 %merge.4 = (bf16[7392,1024]{1,0:T(8,128)(2,1)}, bf16[7392,1024]{1,0:T(8,128)(2,1)}) custom-call(bf16[256,1024]{1,0:T(8,128)(2,1)S(1)} %maximum_select_fusion.3.low, bf16[7392,1024]{1,0:T(8,128)(2,1)} %bitcast.32, bf16[7392,1024]{1,0:T(8,128)(2,1)} %bitcast.38, ...), custom_call_target="tpu_custom_call", output_to_operand_aliasing={{0}: (7, {}), {1}: (8, {})} | custom-call | flops 1024 | bytes 1024 | tf_op jit(solution)/shard_map/merge/pallas_call | solution.py:188
  113.9 1.1 collective-permute-done.25.up_came
  115.2 1.0 collective-permute-start.27
  116.4 1.5 %collective-permute-start.28 = (bf16[48,2560]{1,0:T(8,128)(2,1)S(1)}, bf16[48,2560]{1,0:T(8,128)(2,1)S(1)}, u32[]{:S(2)}, u32[]{:S(2)}) collective-permute-start(bf16[48,2560]{1,0:T(8,128)(2,1)S(1)} %get-tuple-element.480), channel_id=1, source_target_pairs={{0,16},{4,20},{8,24},{12,28},{16,0},{20,4},{24,8},{28,12},{1,17},{... | collective-permute-start | bytes 737288 | tf_op jit(solution)/shard_map/ppermute | solution.py:29
  118.1 2.8 %merge.5 = (bf16[7392,1024]{1,0:T(8,128)(2,1)}, bf16[7392,1024]{1,0:T(8,128)(2,1)}) custom-call(bf16[256,1024]{1,0:T(8,128)(2,1)S(1)} %maximum_select_fusion.3.low, bf16[7392,1024]{1,0:T(8,128)(2,1)} %bitcast.33, bf16[7392,1024]{1,0:T(8,128)(2,1)} %bitcast.39, ...), custom_call_target="tpu_custom_call", output_to_operand_aliasing={{0}: (7, {}), {1}: (8, {})} | custom-call | flops 1024 | bytes 1024 | tf_op jit(solution)/shard_map/merge/pallas_call | solution.py:188
  121.1 1.2 finish.3.refs_0_
  122.3 1.2 finish.4.refs_0_
  123.5 1.2 finish.5
  (85 shorter events, 7.1 us)
Async XLA Ops:
  0.6 14.1 %collective-permute-start = (bf16[96,1024]{1,0:T(8,128)(2,1)}, bf16[96,1024]{1,0:T(8,128)(2,1)}, u32[]{:S(2)}, u32[]{:S(2)}) collective-permute-start(bf16[96,1024]{1,0:T(8,128)(2,1)} %param.10), channel_id=1, source_target_pairs={{0,2},{1,3},{2,0},{3,1},{4,6},{5,7},{6,4},{7,5},{8,10},{9,11},{10,... | collective-permute-start | bytes 589832 | tf_op jit(solution)/shard_map/ppermute | solution.py:29
  7.2 11.0 %collective-permute-start.3 = (bf16[128,1024]{1,0:T(8,128)(2,1)S(1)}, bf16[128,1024]{1,0:T(8,128)(2,1)}, u32[]{:S(2)}, u32[]{:S(2)}) collective-permute-start(bf16[128,1024]{1,0:T(8,128)(2,1)S(1)} %get-tuple-element.499), channel_id=1, source_target_pairs={{0,1},{1,0},{2,3},{3,2},{4,5},{5,4},{6,7},{7,6},{8,9},{9,8},{10,11... | collective-permute-start | bytes 786440 | tf_op jit(solution)/shard_map/ppermute | solution.py:29
  10.5 3.1 %copy-start = (s32[4]{0:T(128)S(1)}, s32[4]{0:T(128)}, u32[]{:S(2)}) copy-start(s32[4]{0:T(128)} %constant.91.clone) | copy-start | bytes 52
  10.5 9.1 %collective-permute-start.1 = (bf16[64,7392]{1,0:T(8,128)(2,1)S(1)}, bf16[64,7392]{1,0:T(8,128)(2,1)}, u32[]{:S(2)}, u32[]{:S(2)}) collective-permute-start(bf16[64,7392]{1,0:T(8,128)(2,1)S(1)} %get-tuple-element.497), channel_id=1, source_target_pairs={{0,4},{4,0},{8,12},{12,8},{16,20},{20,16},{24,28},{28,24},{1,5},{5... | collective-permute-start | bytes 2838536 | tf_op jit(solution)/shard_map/ppermute | solution.py:29
  13.1 6.4 %collective-permute-start.2 = (bf16[64,7392]{1,0:T(8,128)(2,1)}, bf16[64,7392]{1,0:T(8,128)(2,1)}, u32[]{:S(2)}, u32[]{:S(2)}) collective-permute-start(bf16[64,7392]{1,0:T(8,128)(2,1)} %get-tuple-element.495), channel_id=1, source_target_pairs={{0,4},{4,0},{8,12},{12,8},{16,20},{20,16},{24,28},{28,24},{1,5},{5... | collective-permute-start | bytes 2838536 | tf_op jit(solution)/shard_map/ppermute | solution.py:29
  15.7 13.9 %collective-permute-start.4 = (bf16[192,1024]{1,0:T(8,128)(2,1)S(1)}, bf16[192,1024]{1,0:T(8,128)(2,1)S(1)}, u32[]{:S(2)}, u32[]{:S(2)}) collective-permute-start(bf16[192,1024]{1,0:T(8,128)(2,1)S(1)} %constant_dynamic-update-slice_fusion.refs_0_), channel_id=1, source_target_pairs={{0,1},{1,0},{2,3},{3,2},{4,5},{5,4},{6,7},{7,6},{8,9},{9,8},{10,11... | collective-permute-start | bytes 1179656 | tf_op jit(solution)/shard_map/ppermute | solution.py:29
  18.3 11.9 %collective-permute-start.7 = (bf16[64,1024]{1,0:T(8,128)(2,1)S(1)}, bf16[64,1024]{1,0:T(8,128)(2,1)S(1)}, u32[]{:S(2)}, u32[]{:S(2)}) collective-permute-start(bf16[64,1024]{1,0:T(8,128)(2,1)S(1)} %get-tuple-element.522), channel_id=1, source_target_pairs={{0,2},{1,3},{2,0},{3,1},{4,6},{5,7},{6,4},{7,5},{8,10},{9,11},{10,... | collective-permute-start | bytes 393224 | tf_op jit(solution)/shard_map/ppermute | solution.py:29
  19.8 13.7 %collective-permute-start.6 = (bf16[32,7392]{1,0:T(8,128)(2,1)S(1)}, bf16[32,7392]{1,0:T(8,128)(2,1)S(1)}, u32[]{:S(2)}, u32[]{:S(2)}) collective-permute-start(bf16[32,7392]{1,0:T(8,128)(2,1)S(1)} %get-tuple-element.502), channel_id=1, source_target_pairs={{0,16},{4,20},{8,24},{12,28},{16,0},{20,4},{24,8},{28,12},{1,17},{... | collective-permute-start | bytes 1419272 | tf_op jit(solution)/shard_map/ppermute | solution.py:29
  21.5 13.7 %collective-permute-start.5 = (bf16[32,7392]{1,0:T(8,128)(2,1)S(1)}, bf16[32,7392]{1,0:T(8,128)(2,1)S(1)}, u32[]{:S(2)}, u32[]{:S(2)}) collective-permute-start(bf16[32,7392]{1,0:T(8,128)(2,1)S(1)} %get-tuple-element.504), channel_id=1, source_target_pairs={{0,8},{4,12},{8,0},{12,4},{16,24},{20,28},{24,16},{28,20},{1,9},{5... | collective-permute-start | bytes 1419272 | tf_op jit(solution)/shard_map/ppermute | solution.py:29
  30.2 14.6 %collective-permute-start.10 = (bf16[64,1024]{1,0:T(8,128)(2,1)S(1)}, bf16[64,1024]{1,0:T(8,128)(2,1)S(1)}, u32[]{:S(2)}, u32[]{:S(2)}) collective-permute-start(bf16[64,1024]{1,0:T(8,128)(2,1)S(1)} %broadcast_select_fusion.7), channel_id=1, source_target_pairs={{0,2},{1,3},{2,0},{3,1},{4,6},{5,7},{6,4},{7,5},{8,10},{9,11},{10,... | collective-permute-start | bytes 393224 | tf_op jit(solution)/shard_map/ppermute | solution.py:29
  33.6 11.2 %collective-permute-start.9 = (bf16[16,7392]{1,0:T(8,128)(2,1)S(1)}, bf16[16,7392]{1,0:T(8,128)(2,1)S(1)}, u32[]{:S(2)}, u32[]{:S(2)}) collective-permute-start(bf16[16,7392]{1,0:T(8,128)(2,1)S(1)} %get-tuple-element.518), channel_id=1, source_target_pairs={{0,8},{4,12},{8,0},{12,4},{16,24},{20,28},{24,16},{28,20},{1,9},{5... | collective-permute-start | bytes 709640 | tf_op jit(solution)/shard_map/ppermute | solution.py:29
  35.3 9.5 %collective-permute-start.8 = (bf16[16,7392]{1,0:T(8,128)(2,1)S(1)}, bf16[16,7392]{1,0:T(8,128)(2,1)S(1)}, u32[]{:S(2)}, u32[]{:S(2)}) collective-permute-start(bf16[16,7392]{1,0:T(8,128)(2,1)S(1)} %get-tuple-element.520), channel_id=1, source_target_pairs={{0,16},{4,20},{8,24},{12,28},{16,0},{20,4},{24,8},{28,12},{1,17},{... | collective-permute-start | bytes 709640 | tf_op jit(solution)/shard_map/ppermute | solution.py:29
  44.8 4.0 %collective-permute-start.11 = (bf16[384,2560]{1,0:T(8,128)(2,1)S(1)}, bf16[384,2560]{1,0:T(8,128)(2,1)S(1)}, u32[]{:S(2)}, u32[]{:S(2)}) collective-permute-start(bf16[384,2560]{1,0:T(8,128)(2,1)S(1)} %get-tuple-element.261), channel_id=1, source_target_pairs={{0,4},{4,0},{8,12},{12,8},{16,20},{20,16},{24,28},{28,24},{1,5},{5... | collective-permute-start | bytes 5898248 | tf_op jit(solution)/shard_map/ppermute | solution.py:29
  44.9 14.2 %collective-permute-start.13 = (bf16[16,7392]{1,0:T(8,128)(2,1)S(1)}, bf16[16,7392]{1,0:T(8,128)(2,1)S(1)}, u32[]{:S(2)}, u32[]{:S(2)}) collective-permute-start(bf16[16,7392]{1,0:T(8,128)(2,1)S(1)} %broadcast_select_fusion.5), channel_id=1, source_target_pairs={{0,8},{4,12},{8,0},{12,4},{16,24},{20,28},{24,16},{28,20},{1,9},{5... | collective-permute-start | bytes 709640 | tf_op jit(solution)/shard_map/ppermute | solution.py:29
  45.6 13.6 %collective-permute-start.12 = (bf16[16,7392]{1,0:T(8,128)(2,1)S(1)}, bf16[16,7392]{1,0:T(8,128)(2,1)S(1)}, u32[]{:S(2)}, u32[]{:S(2)}) collective-permute-start(bf16[16,7392]{1,0:T(8,128)(2,1)S(1)} %broadcast_select_fusion.6), channel_id=1, source_target_pairs={{0,16},{4,20},{8,24},{12,28},{16,0},{20,4},{24,8},{28,12},{1,17},{... | collective-permute-start | bytes 709640 | tf_op jit(solution)/shard_map/ppermute | solution.py:29
  46.9 12.3 %collective-permute-start.14 = (bf16[128,1024]{1,0:T(8,128)(2,1)S(1)}, bf16[128,1024]{1,0:T(8,128)(2,1)S(1)}, u32[]{:S(2)}, u32[]{:S(2)}) collective-permute-start(bf16[128,1024]{1,0:T(8,128)(2,1)S(1)} %maximum_select_fusion.6), channel_id=1, source_target_pairs={{0,1},{1,0},{2,3},{3,2},{4,5},{5,4},{6,7},{7,6},{8,9},{9,8},{10,11... | collective-permute-start | bytes 786440 | tf_op jit(solution)/shard_map/ppermute | solution.py:29
  49.6 21.1 %collective-permute-start.15 = (bf16[96,2560]{1,0:T(8,128)(2,1)S(1)}, bf16[96,2560]{1,0:T(8,128)(2,1)S(1)}, u32[]{:S(2)}, u32[]{:S(2)}) collective-permute-start(bf16[96,2560]{1,0:T(8,128)(2,1)S(1)} %get-tuple-element.476), channel_id=1, source_target_pairs={{0,8},{4,12},{8,0},{12,4},{16,24},{20,28},{24,16},{28,20},{1,9},{5... | collective-permute-start | bytes 1474568 | tf_op jit(solution)/shard_map/ppermute | solution.py:29
  50.4 20.6 %collective-permute-start.16 = (bf16[96,2560]{1,0:T(8,128)(2,1)S(1)}, bf16[96,2560]{1,0:T(8,128)(2,1)S(1)}, u32[]{:S(2)}, u32[]{:S(2)}) collective-permute-start(bf16[96,2560]{1,0:T(8,128)(2,1)S(1)} %get-tuple-element.474), channel_id=1, source_target_pairs={{0,16},{4,20},{8,24},{12,28},{16,0},{20,4},{24,8},{28,12},{1,17},{... | collective-permute-start | bytes 1474568 | tf_op jit(solution)/shard_map/ppermute | solution.py:29
  59.5 14.8 %collective-permute-start.19 = (bf16[32,7392]{1,0:T(8,128)(2,1)S(1)}, bf16[32,7392]{1,0:T(8,128)(2,1)S(1)}, u32[]{:S(2)}, u32[]{:S(2)}) collective-permute-start(bf16[32,7392]{1,0:T(8,128)(2,1)S(1)} %maximum_select_fusion.5), channel_id=1, source_target_pairs={{0,16},{4,20},{8,24},{12,28},{16,0},{20,4},{24,8},{28,12},{1,17},{... | collective-permute-start | bytes 1419272 | tf_op jit(solution)/shard_map/ppermute | solution.py:29
  61.0 9.9 %collective-permute-start.17 = (bf16[384,2560]{1,0:T(8,128)(2,1)S(1)}, bf16[384,2560]{1,0:T(8,128)(2,1)S(1)}, u32[]{:S(2)}, u32[]{:S(2)}) collective-permute-start(bf16[384,2560]{1,0:T(8,128)(2,1)S(1)} %get-tuple-element.320), channel_id=1, source_target_pairs={{0,4},{4,0},{8,12},{12,8},{16,20},{20,16},{24,28},{28,24},{1,5},{5... | collective-permute-start | bytes 5898248 | tf_op jit(solution)/shard_map/ppermute | solution.py:29
  61.2 13.3 %collective-permute-start.18 = (bf16[32,7392]{1,0:T(8,128)(2,1)S(1)}, bf16[32,7392]{1,0:T(8,128)(2,1)S(1)}, u32[]{:S(2)}, u32[]{:S(2)}) collective-permute-start(bf16[32,7392]{1,0:T(8,128)(2,1)S(1)} %maximum_select_fusion.4), channel_id=1, source_target_pairs={{0,8},{4,12},{8,0},{12,4},{16,24},{20,28},{24,16},{28,20},{1,9},{5... | collective-permute-start | bytes 1419272 | tf_op jit(solution)/shard_map/ppermute | solution.py:29
  70.7 23.2 %collective-permute-start.24 = (bf16[384,2560]{1,0:T(8,128)(2,1)S(1)}, bf16[384,2560]{1,0:T(8,128)(2,1)S(1)}, u32[]{:S(2)}, u32[]{:S(2)}) collective-permute-start(bf16[384,2560]{1,0:T(8,128)(2,1)S(1)} %get-tuple-element.377), channel_id=1, source_target_pairs={{0,4},{4,0},{8,12},{12,8},{16,20},{20,16},{24,28},{28,24},{1,5},{5... | collective-permute-start | bytes 5898248 | tf_op jit(solution)/shard_map/ppermute | solution.py:29
  74.7 2.8 %collective-permute-start.21 = (bf16[64,7392]{1,0:T(8,128)(2,1)S(1)}, bf16[64,7392]{1,0:T(8,128)(2,1)S(1)}, u32[]{:S(2)}, u32[]{:S(2)}) collective-permute-start(bf16[64,7392]{1,0:T(8,128)(2,1)S(1)} %maximum_select_fusion.1.up_b), channel_id=1, source_target_pairs={{0,4},{4,0},{8,12},{12,8},{16,20},{20,16},{24,28},{28,24},{1,5},{5... | collective-permute-start | bytes 2838536 | tf_op jit(solution)/shard_map/ppermute | solution.py:29
  74.9 3.7 %collective-permute-start.20 = (bf16[64,7392]{1,0:T(8,128)(2,1)S(1)}, bf16[64,7392]{1,0:T(8,128)(2,1)S(1)}, u32[]{:S(2)}, u32[]{:S(2)}) collective-permute-start(bf16[64,7392]{1,0:T(8,128)(2,1)S(1)} %maximum_select_fusion.gate_b), channel_id=1, source_target_pairs={{0,4},{4,0},{8,12},{12,8},{16,20},{20,16},{24,28},{28,24},{1,5},{5... | collective-permute-start | bytes 2838536 | tf_op jit(solution)/shard_map/ppermute | solution.py:29
  75.5 18.5 %collective-permute-start.23 = (bf16[144,2560]{1,0:T(8,128)(2,1)S(1)}, bf16[144,2560]{1,0:T(8,128)(2,1)S(1)}, u32[]{:S(2)}, u32[]{:S(2)}) collective-permute-start(bf16[144,2560]{1,0:T(8,128)(2,1)S(1)} %pad_maximum_fusion.1), channel_id=1, source_target_pairs={{0,16},{4,20},{8,24},{12,28},{16,0},{20,4},{24,8},{28,12},{1,17},{... | collective-permute-start | bytes 2211848 | tf_op jit(solution)/shard_map/ppermute | solution.py:29
  76.7 18.2 %collective-permute-start.22 = (bf16[144,2560]{1,0:T(8,128)(2,1)S(1)}, bf16[144,2560]{1,0:T(8,128)(2,1)S(1)}, u32[]{:S(2)}, u32[]{:S(2)}) collective-permute-start(bf16[144,2560]{1,0:T(8,128)(2,1)S(1)} %pad_maximum_fusion), channel_id=1, source_target_pairs={{0,8},{4,12},{8,0},{12,4},{16,24},{20,28},{24,16},{28,20},{1,9},{5... | collective-permute-start | bytes 2211848 | tf_op jit(solution)/shard_map/ppermute | solution.py:29
  96.0 17.9 %collective-permute-start.26 = (bf16[144,2560]{1,0:T(8,128)(2,1)S(1)}, bf16[144,2560]{1,0:T(8,128)(2,1)S(1)}, u32[]{:S(2)}, u32[]{:S(2)}) collective-permute-start(bf16[144,2560]{1,0:T(8,128)(2,1)S(1)} %pad_maximum_fusion.3), channel_id=1, source_target_pairs={{0,16},{4,20},{8,24},{12,28},{16,0},{20,4},{24,8},{28,12},{1,17},{... | collective-permute-start | bytes 2211848 | tf_op jit(solution)/shard_map/ppermute | solution.py:29
  97.3 17.7 %collective-permute-start.25 = (bf16[144,2560]{1,0:T(8,128)(2,1)S(1)}, bf16[144,2560]{1,0:T(8,128)(2,1)S(1)}, u32[]{:S(2)}, u32[]{:S(2)}) collective-permute-start(bf16[144,2560]{1,0:T(8,128)(2,1)S(1)} %pad_maximum_fusion.2), channel_id=1, source_target_pairs={{0,8},{4,12},{8,0},{12,4},{16,24},{20,28},{24,16},{28,20},{1,9},{5... | collective-permute-start | bytes 2211848 | tf_op jit(solution)/shard_map/ppermute | solution.py:29
  115.2 8.2 %collective-permute-start.27 = (bf16[48,2560]{1,0:T(8,128)(2,1)S(1)}, bf16[48,2560]{1,0:T(8,128)(2,1)S(1)}, u32[]{:S(2)}, u32[]{:S(2)}) collective-permute-start(bf16[48,2560]{1,0:T(8,128)(2,1)S(1)} %get-tuple-element.478), channel_id=1, source_target_pairs={{0,8},{4,12},{8,0},{12,4},{16,24},{20,28},{24,16},{28,20},{1,9},{5... | collective-permute-start | bytes 737288 | tf_op jit(solution)/shard_map/ppermute | solution.py:29
  116.4 7.1 %collective-permute-start.28 = (bf16[48,2560]{1,0:T(8,128)(2,1)S(1)}, bf16[48,2560]{1,0:T(8,128)(2,1)S(1)}, u32[]{:S(2)}, u32[]{:S(2)}) collective-permute-start(bf16[48,2560]{1,0:T(8,128)(2,1)S(1)} %get-tuple-element.480), channel_id=1, source_target_pairs={{0,16},{4,20},{8,24},{12,28},{16,0},{20,4},{24,8},{28,12},{1,17},{... | collective-permute-start | bytes 737288 | tf_op jit(solution)/shard_map/ppermute | solution.py:29

commit v3 on v2

--- a/solution.py
+++ b/solution.py
@@ -130,7 +130,7 @@
             pl.BlockSpec((half, TILE), lambda i: (0, i)),
         ],
         compiler_params=pltpu.CompilerParams(
-            dimension_semantics=("arbitrary",), vmem_limit_bytes=40 * 2**20
+            dimension_semantics=("arbitrary",), vmem_limit_bytes=22 * 2**20
         ),
         cost_estimate=COST,
         name="multiply",
@@ -193,7 +193,7 @@
         out_specs=[weight] * 2,
         input_output_aliases={7: 0, 8: 1} if merged else {},
         compiler_params=pltpu.CompilerParams(
-            dimension_semantics=("arbitrary",), vmem_limit_bytes=40 * 2**20
+            dimension_semantics=("arbitrary",), vmem_limit_bytes=22 * 2**20
         ),
         cost_estimate=SMALL,
         name="merge",

time: 125 us -> 124 us (level)
  Pallas kernels: 61 us -> 51.8 us
  waiting for transfers between devices: 17.4 us -> 23 us
  other arithmetic: 6.71 us -> 8.35 us
    pallas_call x3, Pallas kernels: 32.8 us -> 26.1 us  [merge_span(): pl.pallas_call(merge_kernel, grid=(count,), out_shape=[jax.ShapeDtypeStru...]
    ppermute x29, waiting for transfers between devices: 17.4 us -> 23 us  [swap(): return lax.ppermute(value, axis, [(i, i ^ distance) for i in range(size)])]
    pallas_call x3, Pallas kernels: 23.4 us -> 20.9 us  [multiply_chunk(): pl.pallas_call(functools.partial(multiply_kernel, rows, places), grid=(co...]
    select_n x7, other arithmetic: 0.41 us -> 2.05 us  [chosen(): jnp.where(mine == bit(self.owner, self.last), self.held, self.arrived[0])]
  transfers between devices with their start and end apart: 29 -> 29, of which waited for: 10 -> 11; matrix products, arithmetic and copies ran while one was open for 10% -> 11% of each run, Pallas kernels for 48% -> 41%
where the time goes in v3:
time: 124 us; the launch traced here: 123 us
  Pallas kernels  51.8 us (42%)
  starting transfers between devices  30.3 us (24%)
  waiting for transfers between devices  23 us (19%)
  other arithmetic  8.35 us (7%)
  local copies, waits for them, and re-layouts  6.74 us (5%)
  between operations  2.53 us (2%)
    ppermute x29, starting transfers between devices, swap(): return lax.ppermute(value, axis, [(i, i ^ distance) for i in range(size)])  30.3 us
    pallas_call x3, Pallas kernels, merge_span(): pl.pallas_call(merge_kernel, grid=(count,), out_shape=[jax.ShapeDtypeStru...  26.1 us
    ppermute x29, waiting for transfers between devices, swap(): return lax.ppermute(value, axis, [(i, i ^ distance) for i in range(size)])  23 us
    pallas_call x3, Pallas kernels, multiply_chunk(): pl.pallas_call(functools.partial(multiply_kernel, rows, places), grid=(co...  20.9 us
    squeeze x2, local copies, waits for them, and re-layouts, slot(): return lax.dynamic_index_in_dim(stack, i, 0, keepdims=False)  4.32 us
    pallas_call x3, Pallas kernels, finished(): pl.pallas_call(finish_kernel, grid=(1,), out_shape=[jax.ShapeDtypeStruct(...  3.63 us
  transfers between devices with their start and end apart: 29, of which 11 were waited for; matrix products, arithmetic and copies ran while one was open for 11% of the time, Pallas kernels for 41%

profile of v3, /device:TPU:0, one launch (start us, length us, event | category | flops | bytes accessed | tf_op | source)
XLA Modules:
  0.0 122.7 jit_solution(1480776267954015557)
XLA Ops:
  0.6 4.1 %collective-permute-start = (bf16[96,1024]{1,0:T(8,128)(2,1)}, bf16[96,1024]{1,0:T(8,128)(2,1)}, u32[]{:S(2)}, u32[]{:S(2)}) collective-permute-start(bf16[96,1024]{1,0:T(8,128)(2,1)} %param.10), channel_id=1, source_target_pairs={{0,2},{1,3},{2,0},{3,1},{4,6},{5,7},{6,4},{7,5},{8,10},{9,11},{10,... | collective-permute-start | bytes 589832 | tf_op jit(solution)/shard_map/ppermute | solution.py:29
  6.1 1.1 fusion.13
  7.2 1.6 %collective-permute-start.3 = (bf16[128,1024]{1,0:T(8,128)(2,1)S(1)}, bf16[128,1024]{1,0:T(8,128)(2,1)}, u32[]{:S(2)}, u32[]{:S(2)}) collective-permute-start(bf16[128,1024]{1,0:T(8,128)(2,1)S(1)} %get-tuple-element.499), channel_id=1, source_target_pairs={{0,1},{1,0},{2,3},{3,2},{4,5},{5,4},{6,7},{7,6},{8,9},{9,8},{10,11... | collective-permute-start | bytes 786440 | tf_op jit(solution)/shard_map/ppermute | solution.py:29
  8.9 1.6 %dynamic-slice_bitcast_fusion.1 = (bf16[64,7392]{1,0:T(8,128)(2,1)S(1)}, bf16[64,7392]{1,0:T(8,128)(2,1)S(1)}) fusion(bf16[2,64,7392]{2,1,0:T(8,128)(2,1)} %param.15, s32[]{:T(128)S(6)} %select_n.207, s32[]{:T(128)S(6)} %select_n.201), kind=kLoop, calls=%fused_computation.31 | loop fusion | bytes 3784712 | tf_op jit(solution)/shard_map/jit(dynamic_index_in_dim)/squeeze | solution.py:317
  10.6 2.7 %dynamic-slice_bitcast_fusion = (bf16[64,7392]{1,0:T(8,128)(2,1)}, bf16[64,7392]{1,0:T(8,128)(2,1)S(1)}) fusion(bf16[2,64,7392]{2,1,0:T(8,128)(2,1)} %param.16, s32[]{:T(128)S(6)} %select_n.207, s32[]{:T(128)S(6)} %select_n.201), kind=kLoop, calls=%fused_computation.30 | loop fusion | bytes 3784712 | tf_op jit(solution)/shard_map/jit(dynamic_index_in_dim)/squeeze | solution.py:317
  14.0 0.9 constant_dynamic-update-slice_fusion.1
  14.9 0.9 constant_dynamic-update-slice_fusion.refs_0_
  16.4 1.8 %collective-permute-done.3 = bf16[128,1024]{1,0:T(8,128)(2,1)} collective-permute-done((bf16[128,1024]{1,0:T(8,128)(2,1)S(1)}, bf16[128,1024]{1,0:T(8,128)(2,1)}, u32[]{:S(2)}, u32[]{:S(2)}) %collective-permute-start.3) | collective-permute-done | bytes 262176 | tf_op jit(solution)/shard_map/ppermute | solution.py:29
  18.3 1.2 %collective-permute-start.7 = (bf16[64,1024]{1,0:T(8,128)(2,1)S(1)}, bf16[64,1024]{1,0:T(8,128)(2,1)S(1)}, u32[]{:S(2)}, u32[]{:S(2)}) collective-permute-start(bf16[64,1024]{1,0:T(8,128)(2,1)S(1)} %get-tuple-element.522), channel_id=1, source_target_pairs={{0,2},{1,3},{2,0},{3,1},{4,6},{5,7},{6,4},{7,5},{8,10},{9,11},{10,... | collective-permute-start | bytes 393224 | tf_op jit(solution)/shard_map/ppermute | solution.py:29
  19.5 1.8 %broadcast_select_fusion = (bf16[64,7392]{1,0:T(8,128)(2,1)S(1)}, bf16[64,7392]{1,0:T(8,128)(2,1)S(1)}) fusion(bf16[64,7392]{1,0:T(8,128)(2,1)S(1)} %get-tuple-element.235, bf16[64,7392]{1,0:T(8,128)(2,1)} %collective-permute-done.2, pred[]{:T(512)S(6)} %eq.49, bf16[64,7392]{1,0:T(8,128)(2,1)S(1)} %get-tuple-element.234, ...), kind=kLoop, calls=%fused_computation.34 | loop fusion | flops 946176 | bytes 5677057 | tf_op jit(solution)/shard_map/jit(_where)/select_n | solution.py:48
  21.4 1.6 %collective-permute-start.6 = (bf16[32,7392]{1,0:T(8,128)(2,1)S(1)}, bf16[32,7392]{1,0:T(8,128)(2,1)S(1)}, u32[]{:S(2)}, u32[]{:S(2)}) collective-permute-start(bf16[32,7392]{1,0:T(8,128)(2,1)S(1)} %get-tuple-element.502), channel_id=1, source_target_pairs={{0,16},{4,20},{8,24},{12,28},{16,0},{20,4},{24,8},{28,12},{1,17},{... | collective-permute-start | bytes 1419272 | tf_op jit(solution)/shard_map/ppermute | solution.py:29
  23.1 1.6 %collective-permute-start.5 = (bf16[32,7392]{1,0:T(8,128)(2,1)S(1)}, bf16[32,7392]{1,0:T(8,128)(2,1)S(1)}, u32[]{:S(2)}, u32[]{:S(2)}) collective-permute-start(bf16[32,7392]{1,0:T(8,128)(2,1)S(1)} %get-tuple-element.504), channel_id=1, source_target_pairs={{0,8},{4,12},{8,0},{12,4},{16,24},{20,28},{24,16},{28,20},{1,9},{5... | collective-permute-start | bytes 1419272 | tf_op jit(solution)/shard_map/ppermute | solution.py:29
  24.7 5.1 %collective-permute-done.4.refs_1_ = bf16[192,1024]{1,0:T(8,128)(2,1)S(1)} collective-permute-done((bf16[192,1024]{1,0:T(8,128)(2,1)S(1)}, bf16[192,1024]{1,0:T(8,128)(2,1)S(1)}, u32[]{:S(2)}, u32[]{:S(2)}) %collective-permute-start.4) | collective-permute-done | bytes 393248 | tf_op jit(solution)/shard_map/ppermute | solution.py:29
  29.8 0.6 order_tokens.1.tok
  30.4 1.0 collective-permute-start.10
  31.4 2.3 %collective-permute-done.6 = bf16[32,7392]{1,0:T(8,128)(2,1)S(1)} collective-permute-done((bf16[32,7392]{1,0:T(8,128)(2,1)S(1)}, bf16[32,7392]{1,0:T(8,128)(2,1)S(1)}, u32[]{:S(2)}, u32[]{:S(2)}) %collective-permute-start.6) | collective-permute-done | bytes 473120 | tf_op jit(solution)/shard_map/ppermute | solution.py:29
  33.8 1.6 %collective-permute-start.9 = (bf16[16,7392]{1,0:T(8,128)(2,1)S(1)}, bf16[16,7392]{1,0:T(8,128)(2,1)S(1)}, u32[]{:S(2)}, u32[]{:S(2)}) collective-permute-start(bf16[16,7392]{1,0:T(8,128)(2,1)S(1)} %get-tuple-element.518), channel_id=1, source_target_pairs={{0,8},{4,12},{8,0},{12,4},{16,24},{20,28},{24,16},{28,20},{1,9},{5... | collective-permute-start | bytes 709640 | tf_op jit(solution)/shard_map/ppermute | solution.py:29
  35.5 1.6 %collective-permute-start.8 = (bf16[16,7392]{1,0:T(8,128)(2,1)S(1)}, bf16[16,7392]{1,0:T(8,128)(2,1)S(1)}, u32[]{:S(2)}, u32[]{:S(2)}) collective-permute-start(bf16[16,7392]{1,0:T(8,128)(2,1)S(1)} %get-tuple-element.520), channel_id=1, source_target_pairs={{0,16},{4,20},{8,24},{12,28},{16,0},{20,4},{24,8},{28,12},{1,17},{... | collective-permute-start | bytes 709640 | tf_op jit(solution)/shard_map/ppermute | solution.py:29
  37.0 7.0 %multiply.3 = (bf16[384,2560]{1,0:T(8,128)(2,1)S(1)}, f32[192,2560]{1,0:T(8,128)S(1)}, f32[192,2560]{1,0:T(8,128)S(1)}) custom-call(bf16[384,1024]{1,0:T(8,128)(2,1)S(1)} %order_tokens.1.tok, bf16[7392,1024]{1,0:T(8,128)(2,1)S(1)} %bitcast.28, bf16[7392,1024]{1,0:T(8,128)(2,1)} %bitcast.34), custom_call_target="tpu_custom_call" | custom-call | flops 17179869184 | bytes 33554432 | tf_op jit(solution)/shard_map/multiply/pallas_call | solution.py:118
  44.2 0.6 collective-permute-start.13
  44.8 1.3 %collective-permute-start.12 = (bf16[16,7392]{1,0:T(8,128)(2,1)S(1)}, bf16[16,7392]{1,0:T(8,128)(2,1)S(1)}, u32[]{:S(2)}, u32[]{:S(2)}) collective-permute-start(bf16[16,7392]{1,0:T(8,128)(2,1)S(1)} %broadcast_select_fusion.6), channel_id=1, source_target_pairs={{0,16},{4,20},{8,24},{12,28},{16,0},{20,4},{24,8},{28,12},{1,17},{... | collective-permute-start | bytes 709640 | tf_op jit(solution)/shard_map/ppermute | solution.py:29
  46.2 1.1 collective-permute-start.14
  47.2 0.9 collective-permute-done.11
  48.8 0.6 collective-permute-start.15
  49.6 1.3 %collective-permute-start.16 = (bf16[96,2560]{1,0:T(8,128)(2,1)S(1)}, bf16[96,2560]{1,0:T(8,128)(2,1)S(1)}, u32[]{:S(2)}, u32[]{:S(2)}) collective-permute-start(bf16[96,2560]{1,0:T(8,128)(2,1)S(1)} %get-tuple-element.474), channel_id=1, source_target_pairs={{0,16},{4,20},{8,24},{12,28},{16,0},{20,4},{24,8},{28,12},{1,17},{... | collective-permute-start | bytes 1474568 | tf_op jit(solution)/shard_map/ppermute | solution.py:29
  50.9 6.9 %multiply.4 = (bf16[384,2560]{1,0:T(8,128)(2,1)S(1)}, f32[192,2560]{1,0:T(8,128)S(1)}, f32[192,2560]{1,0:T(8,128)S(1)}) custom-call(bf16[384,1024]{1,0:T(8,128)(2,1)S(1)} %order_tokens.1.tok, bf16[7392,1024]{1,0:T(8,128)(2,1)S(1)} %bitcast.29, bf16[7392,1024]{1,0:T(8,128)(2,1)} %bitcast.35), custom_call_target="tpu_custom_call" | custom-call | flops 17179869184 | bytes 33554432 | tf_op jit(solution)/shard_map/multiply/pallas_call | solution.py:118
  58.1 0.9 collective-permute-start.19
  59.0 0.6 multiply_lower.1
  59.8 1.5 %collective-permute-start.18 = (bf16[32,7392]{1,0:T(8,128)(2,1)S(1)}, bf16[32,7392]{1,0:T(8,128)(2,1)S(1)}, u32[]{:S(2)}, u32[]{:S(2)}) collective-permute-start(bf16[32,7392]{1,0:T(8,128)(2,1)S(1)} %maximum_select_fusion.4), channel_id=1, source_target_pairs={{0,8},{4,12},{8,0},{12,4},{16,24},{20,28},{24,16},{28,20},{1,9},{5... | collective-permute-start | bytes 1419272 | tf_op jit(solution)/shard_map/ppermute | solution.py:29
  61.3 7.0 %multiply.5 = (bf16[384,2560]{1,0:T(8,128)(2,1)S(1)}, f32[192,2560]{1,0:T(8,128)S(1)}, f32[192,2560]{1,0:T(8,128)S(1)}) custom-call(bf16[384,1024]{1,0:T(8,128)(2,1)S(1)} %order_tokens.1.tok, bf16[7392,1024]{1,0:T(8,128)(2,1)S(1)} %bitcast.30, bf16[7392,1024]{1,0:T(8,128)(2,1)} %bitcast.36), custom_call_target="tpu_custom_call" | custom-call | flops 17179869184 | bytes 33554432 | tf_op jit(solution)/shard_map/multiply/pallas_call | solution.py:118
  70.1 3.4 %collective-permute-done.19 = bf16[32,7392]{1,0:T(8,128)(2,1)S(1)} collective-permute-done((bf16[32,7392]{1,0:T(8,128)(2,1)S(1)}, bf16[32,7392]{1,0:T(8,128)(2,1)S(1)}, u32[]{:S(2)}, u32[]{:S(2)}) %collective-permute-start.19) | collective-permute-done | bytes 473120 | tf_op jit(solution)/shard_map/ppermute | solution.py:29
  74.5 1.2 %collective-permute-start.23 = (bf16[144,2560]{1,0:T(8,128)(2,1)S(1)}, bf16[144,2560]{1,0:T(8,128)(2,1)S(1)}, u32[]{:S(2)}, u32[]{:S(2)}) collective-permute-start(bf16[144,2560]{1,0:T(8,128)(2,1)S(1)} %pad_maximum_fusion.1), channel_id=1, source_target_pairs={{0,16},{4,20},{8,24},{12,28},{16,0},{20,4},{24,8},{28,12},{1,17},{... | collective-permute-start | bytes 2211848 | tf_op jit(solution)/shard_map/ppermute | solution.py:29
  75.7 0.8 collective-permute-start.22
  76.5 1.1 collective-permute-done.20.gate_c
  77.9 11.7 %merge.3 = (bf16[7392,1024]{1,0:T(8,128)(2,1)}, bf16[7392,1024]{1,0:T(8,128)(2,1)}) custom-call(bf16[256,1024]{1,0:T(8,128)(2,1)S(1)} %maximum_select_fusion.3.low, bf16[7392,1024]{1,0:T(8,128)(2,1)S(1)} %bitcast.31, bf16[7392,1024]{1,0:T(8,128)(2,1)} %bitcast.37, bf16[64,7392]{1,0:T(8,128)(2,1)S(1)} %maximum_select_fusion.gate_b, ...), custom_call_target="tpu_custom_call" | custom-call | flops 1024 | bytes 1024 | tf_op jit(solution)/shard_map/merge/pallas_call | solution.py:188
  89.6 3.3 %collective-permute-done.23.gate_came = bf16[144,2560]{1,0:T(8,128)(2,1)S(1)} collective-permute-done((bf16[144,2560]{1,0:T(8,128)(2,1)S(1)}, bf16[144,2560]{1,0:T(8,128)(2,1)S(1)}, u32[]{:S(2)}, u32[]{:S(2)}) %collective-permute-start.23) | collective-permute-done | bytes 737312 | tf_op jit(solution)/shard_map/ppermute | solution.py:29
  92.9 0.9 collective-permute-done.22.up_came
  94.9 0.9 collective-permute-start.26
  96.2 1.6 %collective-permute-start.25 = (bf16[144,2560]{1,0:T(8,128)(2,1)S(1)}, bf16[144,2560]{1,0:T(8,128)(2,1)S(1)}, u32[]{:S(2)}, u32[]{:S(2)}) collective-permute-start(bf16[144,2560]{1,0:T(8,128)(2,1)S(1)} %pad_maximum_fusion.2), channel_id=1, source_target_pairs={{0,8},{4,12},{8,0},{12,4},{16,24},{20,28},{24,16},{28,20},{1,9},{5... | collective-permute-start | bytes 2211848 | tf_op jit(solution)/shard_map/ppermute | solution.py:29
  97.7 11.7 %merge.4 = (bf16[7392,1024]{1,0:T(8,128)(2,1)}, bf16[7392,1024]{1,0:T(8,128)(2,1)}) custom-call(bf16[256,1024]{1,0:T(8,128)(2,1)S(1)} %maximum_select_fusion.3.low, bf16[7392,1024]{1,0:T(8,128)(2,1)S(1)} %bitcast.32, bf16[7392,1024]{1,0:T(8,128)(2,1)} %bitcast.38, ...), custom_call_target="tpu_custom_call", output_to_operand_aliasing={{0}: (7, {}), {1}: (8, {})} | custom-call | flops 1024 | bytes 1024 | tf_op jit(solution)/shard_map/merge/pallas_call | solution.py:188
  109.4 2.9 %collective-permute-done.26.gate_came = bf16[144,2560]{1,0:T(8,128)(2,1)S(1)} collective-permute-done((bf16[144,2560]{1,0:T(8,128)(2,1)S(1)}, bf16[144,2560]{1,0:T(8,128)(2,1)S(1)}, u32[]{:S(2)}, u32[]{:S(2)}) %collective-permute-start.26) | collective-permute-done | bytes 737312 | tf_op jit(solution)/shard_map/ppermute | solution.py:29
  112.3 1.0 collective-permute-done.25.up_came
  113.5 1.6 %collective-permute-start.27 = (bf16[48,2560]{1,0:T(8,128)(2,1)S(1)}, bf16[48,2560]{1,0:T(8,128)(2,1)S(1)}, u32[]{:S(2)}, u32[]{:S(2)}) collective-permute-start(bf16[48,2560]{1,0:T(8,128)(2,1)S(1)} %get-tuple-element.478), channel_id=1, source_target_pairs={{0,8},{4,12},{8,0},{12,4},{16,24},{20,28},{24,16},{28,20},{1,9},{5... | collective-permute-start | bytes 737288 | tf_op jit(solution)/shard_map/ppermute | solution.py:29
  115.2 0.7 collective-permute-start.28
  116.1 2.7 %merge.5 = (bf16[7392,1024]{1,0:T(8,128)(2,1)}, bf16[7392,1024]{1,0:T(8,128)(2,1)}) custom-call(bf16[256,1024]{1,0:T(8,128)(2,1)S(1)} %maximum_select_fusion.3.low, bf16[7392,1024]{1,0:T(8,128)(2,1)S(1)} %bitcast.33, bf16[7392,1024]{1,0:T(8,128)(2,1)} %bitcast.39, ...), custom_call_target="tpu_custom_call", output_to_operand_aliasing={{0}: (7, {}), {1}: (8, {})} | custom-call | flops 1024 | bytes 1024 | tf_op jit(solution)/shard_map/merge/pallas_call | solution.py:188
  118.9 1.2 finish.3.refs_0_
  120.2 1.2 finish.4.refs_0_
  121.5 1.2 finish.5
  (87 shorter events, 8.2 us)
Async XLA Ops:
  0.6 14.3 %collective-permute-start = (bf16[96,1024]{1,0:T(8,128)(2,1)}, bf16[96,1024]{1,0:T(8,128)(2,1)}, u32[]{:S(2)}, u32[]{:S(2)}) collective-permute-start(bf16[96,1024]{1,0:T(8,128)(2,1)} %param.10), channel_id=1, source_target_pairs={{0,2},{1,3},{2,0},{3,1},{4,6},{5,7},{6,4},{7,5},{8,10},{9,11},{10,... | collective-permute-start | bytes 589832 | tf_op jit(solution)/shard_map/ppermute | solution.py:29
  7.2 11.0 %collective-permute-start.3 = (bf16[128,1024]{1,0:T(8,128)(2,1)S(1)}, bf16[128,1024]{1,0:T(8,128)(2,1)}, u32[]{:S(2)}, u32[]{:S(2)}) collective-permute-start(bf16[128,1024]{1,0:T(8,128)(2,1)S(1)} %get-tuple-element.499), channel_id=1, source_target_pairs={{0,1},{1,0},{2,3},{3,2},{4,5},{5,4},{6,7},{7,6},{8,9},{9,8},{10,11... | collective-permute-start | bytes 786440 | tf_op jit(solution)/shard_map/ppermute | solution.py:29
  10.5 3.3 %copy-start.1 = (s32[4]{0:T(128)S(1)}, s32[4]{0:T(128)}, u32[]{:S(2)}) copy-start(s32[4]{0:T(128)} %constant.91.clone) | copy-start | bytes 52
  10.5 9.1 %collective-permute-start.1 = (bf16[64,7392]{1,0:T(8,128)(2,1)S(1)}, bf16[64,7392]{1,0:T(8,128)(2,1)}, u32[]{:S(2)}, u32[]{:S(2)}) collective-permute-start(bf16[64,7392]{1,0:T(8,128)(2,1)S(1)} %get-tuple-element.497), channel_id=1, source_target_pairs={{0,4},{4,0},{8,12},{12,8},{16,20},{20,16},{24,28},{28,24},{1,5},{5... | collective-permute-start | bytes 2838536 | tf_op jit(solution)/shard_map/ppermute | solution.py:29
  13.3 6.3 %collective-permute-start.2 = (bf16[64,7392]{1,0:T(8,128)(2,1)}, bf16[64,7392]{1,0:T(8,128)(2,1)}, u32[]{:S(2)}, u32[]{:S(2)}) collective-permute-start(bf16[64,7392]{1,0:T(8,128)(2,1)} %get-tuple-element.495), channel_id=1, source_target_pairs={{0,4},{4,0},{8,12},{12,8},{16,20},{20,16},{24,28},{28,24},{1,5},{5... | collective-permute-start | bytes 2838536 | tf_op jit(solution)/shard_map/ppermute | solution.py:29
  15.9 13.9 %collective-permute-start.4 = (bf16[192,1024]{1,0:T(8,128)(2,1)S(1)}, bf16[192,1024]{1,0:T(8,128)(2,1)S(1)}, u32[]{:S(2)}, u32[]{:S(2)}) collective-permute-start(bf16[192,1024]{1,0:T(8,128)(2,1)S(1)} %constant_dynamic-update-slice_fusion.refs_0_), channel_id=1, source_target_pairs={{0,1},{1,0},{2,3},{3,2},{4,5},{5,4},{6,7},{7,6},{8,9},{9,8},{10,11... | collective-permute-start | bytes 1179656 | tf_op jit(solution)/shard_map/ppermute | solution.py:29
  18.3 12.1 %collective-permute-start.7 = (bf16[64,1024]{1,0:T(8,128)(2,1)S(1)}, bf16[64,1024]{1,0:T(8,128)(2,1)S(1)}, u32[]{:S(2)}, u32[]{:S(2)}) collective-permute-start(bf16[64,1024]{1,0:T(8,128)(2,1)S(1)} %get-tuple-element.522), channel_id=1, source_target_pairs={{0,2},{1,3},{2,0},{3,1},{4,6},{5,7},{6,4},{7,5},{8,10},{9,11},{10,... | collective-permute-start | bytes 393224 | tf_op jit(solution)/shard_map/ppermute | solution.py:29
  19.5 17.5 %copy-start = (bf16[1024,7392]{0,1:T(8,128)(2,1)S(1)}, bf16[1024,7392]{0,1:T(8,128)(2,1)}, u32[]{:S(2)}) copy-start(bf16[1024,7392]{0,1:T(8,128)(2,1)} %param.11) | copy-start | bytes 45416452
  21.4 12.2 %collective-permute-start.6 = (bf16[32,7392]{1,0:T(8,128)(2,1)S(1)}, bf16[32,7392]{1,0:T(8,128)(2,1)S(1)}, u32[]{:S(2)}, u32[]{:S(2)}) collective-permute-start(bf16[32,7392]{1,0:T(8,128)(2,1)S(1)} %get-tuple-element.502), channel_id=1, source_target_pairs={{0,16},{4,20},{8,24},{12,28},{16,0},{20,4},{24,8},{28,12},{1,17},{... | collective-permute-start | bytes 1419272 | tf_op jit(solution)/shard_map/ppermute | solution.py:29
  23.1 12.3 %collective-permute-start.5 = (bf16[32,7392]{1,0:T(8,128)(2,1)S(1)}, bf16[32,7392]{1,0:T(8,128)(2,1)S(1)}, u32[]{:S(2)}, u32[]{:S(2)}) collective-permute-start(bf16[32,7392]{1,0:T(8,128)(2,1)S(1)} %get-tuple-element.504), channel_id=1, source_target_pairs={{0,8},{4,12},{8,0},{12,4},{16,24},{20,28},{24,16},{28,20},{1,9},{5... | collective-permute-start | bytes 1419272 | tf_op jit(solution)/shard_map/ppermute | solution.py:29
  30.4 13.6 %collective-permute-start.10 = (bf16[64,1024]{1,0:T(8,128)(2,1)S(1)}, bf16[64,1024]{1,0:T(8,128)(2,1)S(1)}, u32[]{:S(2)}, u32[]{:S(2)}) collective-permute-start(bf16[64,1024]{1,0:T(8,128)(2,1)S(1)} %broadcast_select_fusion.7), channel_id=1, source_target_pairs={{0,2},{1,3},{2,0},{3,1},{4,6},{5,7},{6,4},{7,5},{8,10},{9,11},{10,... | collective-permute-start | bytes 393224 | tf_op jit(solution)/shard_map/ppermute | solution.py:29
  33.8 10.3 %collective-permute-start.9 = (bf16[16,7392]{1,0:T(8,128)(2,1)S(1)}, bf16[16,7392]{1,0:T(8,128)(2,1)S(1)}, u32[]{:S(2)}, u32[]{:S(2)}) collective-permute-start(bf16[16,7392]{1,0:T(8,128)(2,1)S(1)} %get-tuple-element.518), channel_id=1, source_target_pairs={{0,8},{4,12},{8,0},{12,4},{16,24},{20,28},{24,16},{28,20},{1,9},{5... | collective-permute-start | bytes 709640 | tf_op jit(solution)/shard_map/ppermute | solution.py:29
  35.5 8.6 %collective-permute-start.8 = (bf16[16,7392]{1,0:T(8,128)(2,1)S(1)}, bf16[16,7392]{1,0:T(8,128)(2,1)S(1)}, u32[]{:S(2)}, u32[]{:S(2)}) collective-permute-start(bf16[16,7392]{1,0:T(8,128)(2,1)S(1)} %get-tuple-element.520), channel_id=1, source_target_pairs={{0,16},{4,20},{8,24},{12,28},{16,0},{20,4},{24,8},{28,12},{1,17},{... | collective-permute-start | bytes 709640 | tf_op jit(solution)/shard_map/ppermute | solution.py:29
  44.1 4.0 %collective-permute-start.11 = (bf16[384,2560]{1,0:T(8,128)(2,1)S(1)}, bf16[384,2560]{1,0:T(8,128)(2,1)S(1)}, u32[]{:S(2)}, u32[]{:S(2)}) collective-permute-start(bf16[384,2560]{1,0:T(8,128)(2,1)S(1)} %get-tuple-element.261), channel_id=1, source_target_pairs={{0,4},{4,0},{8,12},{12,8},{16,20},{20,16},{24,28},{28,24},{1,5},{5... | collective-permute-start | bytes 5898248 | tf_op jit(solution)/shard_map/ppermute | solution.py:29
  44.2 13.6 %collective-permute-start.13 = (bf16[16,7392]{1,0:T(8,128)(2,1)S(1)}, bf16[16,7392]{1,0:T(8,128)(2,1)S(1)}, u32[]{:S(2)}, u32[]{:S(2)}) collective-permute-start(bf16[16,7392]{1,0:T(8,128)(2,1)S(1)} %broadcast_select_fusion.5), channel_id=1, source_target_pairs={{0,8},{4,12},{8,0},{12,4},{16,24},{20,28},{24,16},{28,20},{1,9},{5... | collective-permute-start | bytes 709640 | tf_op jit(solution)/shard_map/ppermute | solution.py:29
  44.8 13.0 %collective-permute-start.12 = (bf16[16,7392]{1,0:T(8,128)(2,1)S(1)}, bf16[16,7392]{1,0:T(8,128)(2,1)S(1)}, u32[]{:S(2)}, u32[]{:S(2)}) collective-permute-start(bf16[16,7392]{1,0:T(8,128)(2,1)S(1)} %broadcast_select_fusion.6), channel_id=1, source_target_pairs={{0,16},{4,20},{8,24},{12,28},{16,0},{20,4},{24,8},{28,12},{1,17},{... | collective-permute-start | bytes 709640 | tf_op jit(solution)/shard_map/ppermute | solution.py:29
  46.2 11.7 %collective-permute-start.14 = (bf16[128,1024]{1,0:T(8,128)(2,1)S(1)}, bf16[128,1024]{1,0:T(8,128)(2,1)S(1)}, u32[]{:S(2)}, u32[]{:S(2)}) collective-permute-start(bf16[128,1024]{1,0:T(8,128)(2,1)S(1)} %maximum_select_fusion.6), channel_id=1, source_target_pairs={{0,1},{1,0},{2,3},{3,2},{4,5},{5,4},{6,7},{7,6},{8,9},{9,8},{10,11... | collective-permute-start | bytes 786440 | tf_op jit(solution)/shard_map/ppermute | solution.py:29
  48.8 19.6 %collective-permute-start.15 = (bf16[96,2560]{1,0:T(8,128)(2,1)S(1)}, bf16[96,2560]{1,0:T(8,128)(2,1)S(1)}, u32[]{:S(2)}, u32[]{:S(2)}) collective-permute-start(bf16[96,2560]{1,0:T(8,128)(2,1)S(1)} %get-tuple-element.476), channel_id=1, source_target_pairs={{0,8},{4,12},{8,0},{12,4},{16,24},{20,28},{24,16},{28,20},{1,9},{5... | collective-permute-start | bytes 1474568 | tf_op jit(solution)/shard_map/ppermute | solution.py:29
  49.6 19.0 %collective-permute-start.16 = (bf16[96,2560]{1,0:T(8,128)(2,1)S(1)}, bf16[96,2560]{1,0:T(8,128)(2,1)S(1)}, u32[]{:S(2)}, u32[]{:S(2)}) collective-permute-start(bf16[96,2560]{1,0:T(8,128)(2,1)S(1)} %get-tuple-element.474), channel_id=1, source_target_pairs={{0,16},{4,20},{8,24},{12,28},{16,0},{20,4},{24,8},{28,12},{1,17},{... | collective-permute-start | bytes 1474568 | tf_op jit(solution)/shard_map/ppermute | solution.py:29
  58.1 15.4 %collective-permute-start.19 = (bf16[32,7392]{1,0:T(8,128)(2,1)S(1)}, bf16[32,7392]{1,0:T(8,128)(2,1)S(1)}, u32[]{:S(2)}, u32[]{:S(2)}) collective-permute-start(bf16[32,7392]{1,0:T(8,128)(2,1)S(1)} %maximum_select_fusion.5), channel_id=1, source_target_pairs={{0,16},{4,20},{8,24},{12,28},{16,0},{20,4},{24,8},{28,12},{1,17},{... | collective-permute-start | bytes 1419272 | tf_op jit(solution)/shard_map/ppermute | solution.py:29
  59.6 9.0 %collective-permute-start.17 = (bf16[384,2560]{1,0:T(8,128)(2,1)S(1)}, bf16[384,2560]{1,0:T(8,128)(2,1)S(1)}, u32[]{:S(2)}, u32[]{:S(2)}) collective-permute-start(bf16[384,2560]{1,0:T(8,128)(2,1)S(1)} %get-tuple-element.320), channel_id=1, source_target_pairs={{0,4},{4,0},{8,12},{12,8},{16,20},{20,16},{24,28},{28,24},{1,5},{5... | collective-permute-start | bytes 5898248 | tf_op jit(solution)/shard_map/ppermute | solution.py:29
  59.8 13.7 %collective-permute-start.18 = (bf16[32,7392]{1,0:T(8,128)(2,1)S(1)}, bf16[32,7392]{1,0:T(8,128)(2,1)S(1)}, u32[]{:S(2)}, u32[]{:S(2)}) collective-permute-start(bf16[32,7392]{1,0:T(8,128)(2,1)S(1)} %maximum_select_fusion.4), channel_id=1, source_target_pairs={{0,8},{4,12},{8,0},{12,4},{16,24},{20,28},{24,16},{28,20},{1,9},{5... | collective-permute-start | bytes 1419272 | tf_op jit(solution)/shard_map/ppermute | solution.py:29
  68.4 21.2 %collective-permute-start.24 = (bf16[384,2560]{1,0:T(8,128)(2,1)S(1)}, bf16[384,2560]{1,0:T(8,128)(2,1)S(1)}, u32[]{:S(2)}, u32[]{:S(2)}) collective-permute-start(bf16[384,2560]{1,0:T(8,128)(2,1)S(1)} %get-tuple-element.377), channel_id=1, source_target_pairs={{0,4},{4,0},{8,12},{12,8},{16,20},{20,16},{24,28},{28,24},{1,5},{5... | collective-permute-start | bytes 5898248 | tf_op jit(solution)/shard_map/ppermute | solution.py:29
  73.7 2.8 %collective-permute-start.21 = (bf16[64,7392]{1,0:T(8,128)(2,1)S(1)}, bf16[64,7392]{1,0:T(8,128)(2,1)S(1)}, u32[]{:S(2)}, u32[]{:S(2)}) collective-permute-start(bf16[64,7392]{1,0:T(8,128)(2,1)S(1)} %maximum_select_fusion.1.up_b), channel_id=1, source_target_pairs={{0,4},{4,0},{8,12},{12,8},{16,20},{20,16},{24,28},{28,24},{1,5},{5... | collective-permute-start | bytes 2838536 | tf_op jit(solution)/shard_map/ppermute | solution.py:29
  73.9 3.7 %collective-permute-start.20 = (bf16[64,7392]{1,0:T(8,128)(2,1)S(1)}, bf16[64,7392]{1,0:T(8,128)(2,1)S(1)}, u32[]{:S(2)}, u32[]{:S(2)}) collective-permute-start(bf16[64,7392]{1,0:T(8,128)(2,1)S(1)} %maximum_select_fusion.gate_b), channel_id=1, source_target_pairs={{0,4},{4,0},{8,12},{12,8},{16,20},{20,16},{24,28},{28,24},{1,5},{5... | collective-permute-start | bytes 2838536 | tf_op jit(solution)/shard_map/ppermute | solution.py:29
  74.5 18.5 %collective-permute-start.23 = (bf16[144,2560]{1,0:T(8,128)(2,1)S(1)}, bf16[144,2560]{1,0:T(8,128)(2,1)S(1)}, u32[]{:S(2)}, u32[]{:S(2)}) collective-permute-start(bf16[144,2560]{1,0:T(8,128)(2,1)S(1)} %pad_maximum_fusion.1), channel_id=1, source_target_pairs={{0,16},{4,20},{8,24},{12,28},{16,0},{20,4},{24,8},{28,12},{1,17},{... | collective-permute-start | bytes 2211848 | tf_op jit(solution)/shard_map/ppermute | solution.py:29
  75.7 18.2 %collective-permute-start.22 = (bf16[144,2560]{1,0:T(8,128)(2,1)S(1)}, bf16[144,2560]{1,0:T(8,128)(2,1)S(1)}, u32[]{:S(2)}, u32[]{:S(2)}) collective-permute-start(bf16[144,2560]{1,0:T(8,128)(2,1)S(1)} %pad_maximum_fusion), channel_id=1, source_target_pairs={{0,8},{4,12},{8,0},{12,4},{16,24},{20,28},{24,16},{28,20},{1,9},{5... | collective-permute-start | bytes 2211848 | tf_op jit(solution)/shard_map/ppermute | solution.py:29
  94.9 17.4 %collective-permute-start.26 = (bf16[144,2560]{1,0:T(8,128)(2,1)S(1)}, bf16[144,2560]{1,0:T(8,128)(2,1)S(1)}, u32[]{:S(2)}, u32[]{:S(2)}) collective-permute-start(bf16[144,2560]{1,0:T(8,128)(2,1)S(1)} %pad_maximum_fusion.3), channel_id=1, source_target_pairs={{0,16},{4,20},{8,24},{12,28},{16,0},{20,4},{24,8},{28,12},{1,17},{... | collective-permute-start | bytes 2211848 | tf_op jit(solution)/shard_map/ppermute | solution.py:29
  96.2 17.1 %collective-permute-start.25 = (bf16[144,2560]{1,0:T(8,128)(2,1)S(1)}, bf16[144,2560]{1,0:T(8,128)(2,1)S(1)}, u32[]{:S(2)}, u32[]{:S(2)}) collective-permute-start(bf16[144,2560]{1,0:T(8,128)(2,1)S(1)} %pad_maximum_fusion.2), channel_id=1, source_target_pairs={{0,8},{4,12},{8,0},{12,4},{16,24},{20,28},{24,16},{28,20},{1,9},{5... | collective-permute-start | bytes 2211848 | tf_op jit(solution)/shard_map/ppermute | solution.py:29
  113.5 7.9 %collective-permute-start.27 = (bf16[48,2560]{1,0:T(8,128)(2,1)S(1)}, bf16[48,2560]{1,0:T(8,128)(2,1)S(1)}, u32[]{:S(2)}, u32[]{:S(2)}) collective-permute-start(bf16[48,2560]{1,0:T(8,128)(2,1)S(1)} %get-tuple-element.478), channel_id=1, source_target_pairs={{0,8},{4,12},{8,0},{12,4},{16,24},{20,28},{24,16},{28,20},{1,9},{5... | collective-permute-start | bytes 737288 | tf_op jit(solution)/shard_map/ppermute | solution.py:29
  115.2 6.3 %collective-permute-start.28 = (bf16[48,2560]{1,0:T(8,128)(2,1)S(1)}, bf16[48,2560]{1,0:T(8,128)(2,1)S(1)}, u32[]{:S(2)}, u32[]{:S(2)}) collective-permute-start(bf16[48,2560]{1,0:T(8,128)(2,1)S(1)} %get-tuple-element.480), channel_id=1, source_target_pairs={{0,16},{4,20},{8,24},{12,28},{16,0},{20,4},{24,8},{28,12},{1,17},{... | collective-permute-start | bytes 737288 | tf_op jit(solution)/shard_map/ppermute | solution.py:29

commit v4 on v3

--- a/solution.py
+++ b/solution.py
@@ -418,8 +418,7 @@
     state["uppers"] = [part for f in uppers for part in (f.held, f.arrived[0])]
     state["low"] = by_core(state["low"], 0)
     fence()
-    small = pl.cdiv(used, 16)
-    cuts = [0, (used - small + 1) // 2, used - small, used]
+    cuts = [0, (used + 1) // 2, used, used]
     def finish(chosen, hidden):
         if chosen and "correction" not in state:
             ends = sums[turns[min(1, len(turns) - 1)]].finish()
@@ -431,10 +430,11 @@
 
     state["merged"] = []
     for first, last in zip(cuts, cuts[1:]):
-        state["merged"] = merge_span(
-            (first, last - first), weights, state["low"], state["uppers"], state["merged"]
-        )
-        if last == used:
+        if last > first:
+            state["merged"] = merge_span(
+                (first, last - first), weights, state["low"], state["uppers"], state["merged"]
+            )
+        else:
             early = [t for t in turns[:-1] if all(sums[i].step == stages for i in turns[:-1])]
             state["hidden"] = finish(early, [])
         fence(*flying, *[sums[turn] for turn in turns[2:] if sums[turn].step == 0])

time: 124 us -> 124 us (level)
  waiting for transfers between devices: 23 us -> 26.1 us
  Pallas kernels: 51.8 us -> 49.1 us
  starting transfers between devices: 30.3 us -> 28.6 us
    ppermute x29, waiting for transfers between devices: 23 us -> 26.1 us  [swap(): return lax.ppermute(value, axis, [(i, i ^ distance) for i in range(size)])]
    pallas_call x3 -> x2, Pallas kernels: 26.1 us -> 23.4 us  [merge_span(): pl.pallas_call(merge_kernel, grid=(count,), out_shape=[jax.ShapeDtypeStru...]
    ppermute x29, starting transfers between devices: 30.3 us -> 28.6 us  [swap(): return lax.ppermute(value, axis, [(i, i ^ distance) for i in range(size)])]
  transfers between devices with their start and end apart: 29 -> 29, of which waited for: 11 -> 13; matrix products, arithmetic and copies ran while one was open for 11% -> 12% of each run, Pallas kernels for 41% -> 39%
where the time goes in v4:
time: 124 us; the launch traced here: 122 us
  Pallas kernels  49.1 us (40%)
  starting transfers between devices  28.6 us (23%)
  waiting for transfers between devices  26.1 us (21%)
  other arithmetic  9.29 us (7%)
  local copies, waits for them, and re-layouts  6.56 us (5%)
  between operations  2.53 us (2%)
    ppermute x29, starting transfers between devices, swap(): return lax.ppermute(value, axis, [(i, i ^ distance) for i in range(size)])  28.6 us
    ppermute x29, waiting for transfers between devices, swap(): return lax.ppermute(value, axis, [(i, i ^ distance) for i in range(size)])  26.1 us
    pallas_call x2, Pallas kernels, merge_span(): pl.pallas_call(merge_kernel, grid=(count,), out_shape=[jax.ShapeDtypeStru...  23.4 us
    pallas_call x3, Pallas kernels, multiply_chunk(): pl.pallas_call(functools.partial(multiply_kernel, rows, places), grid=(co...  20.9 us
    squeeze x2, local copies, waits for them, and re-layouts, slot(): return lax.dynamic_index_in_dim(stack, i, 0, keepdims=False)  4.14 us
    pallas_call x3, Pallas kernels, finished(): pl.pallas_call(finish_kernel, grid=(1,), out_shape=[jax.ShapeDtypeStruct(...  3.63 us
    select_n x7, other arithmetic, chosen(): jnp.where(mine == bit(self.owner, self.last), self.held, self.arrived[0])  2.99 us
  transfers between devices with their start and end apart: 29, of which 13 were waited for; matrix products, arithmetic and copies ran while one was open for 12% of the time, Pallas kernels for 39%

profile of v4, /device:TPU:0, one launch (start us, length us, event | category | flops | bytes accessed | tf_op | source)
XLA Modules:
  0.0 122.2 jit_solution(1090068460327684262)
XLA Ops:
  0.6 4.1 %collective-permute-start = (bf16[96,1024]{1,0:T(8,128)(2,1)}, bf16[96,1024]{1,0:T(8,128)(2,1)}, u32[]{:S(2)}, u32[]{:S(2)}) collective-permute-start(bf16[96,1024]{1,0:T(8,128)(2,1)} %param.10), channel_id=1, source_target_pairs={{0,2},{1,3},{2,0},{3,1},{4,6},{5,7},{6,4},{7,5},{8,10},{9,11},{10,... | collective-permute-start | bytes 589832 | tf_op jit(solution)/shard_map/ppermute | solution.py:29
  6.1 1.1 fusion.13
  7.2 1.6 %collective-permute-start.3 = (bf16[128,1024]{1,0:T(8,128)(2,1)S(1)}, bf16[128,1024]{1,0:T(8,128)(2,1)}, u32[]{:S(2)}, u32[]{:S(2)}) collective-permute-start(bf16[128,1024]{1,0:T(8,128)(2,1)S(1)} %get-tuple-element.491), channel_id=1, source_target_pairs={{0,1},{1,0},{2,3},{3,2},{4,5},{5,4},{6,7},{7,6},{8,9},{9,8},{10,11... | collective-permute-start | bytes 786440 | tf_op jit(solution)/shard_map/ppermute | solution.py:29
  8.9 1.6 %dynamic-slice_bitcast_fusion.1 = (bf16[64,7392]{1,0:T(8,128)(2,1)S(1)}, bf16[64,7392]{1,0:T(8,128)(2,1)S(1)}) fusion(bf16[2,64,7392]{2,1,0:T(8,128)(2,1)} %param.15, s32[]{:T(128)S(6)} %select_n.207, s32[]{:T(128)S(6)} %select_n.201), kind=kLoop, calls=%fused_computation.31 | loop fusion | bytes 3784712 | tf_op jit(solution)/shard_map/jit(dynamic_index_in_dim)/squeeze | solution.py:317
  10.6 2.5 %dynamic-slice_bitcast_fusion = (bf16[64,7392]{1,0:T(8,128)(2,1)}, bf16[64,7392]{1,0:T(8,128)(2,1)S(1)}) fusion(bf16[2,64,7392]{2,1,0:T(8,128)(2,1)} %param.16, s32[]{:T(128)S(6)} %select_n.207, s32[]{:T(128)S(6)} %select_n.201), kind=kLoop, calls=%fused_computation.30 | loop fusion | bytes 3784712 | tf_op jit(solution)/shard_map/jit(dynamic_index_in_dim)/squeeze | solution.py:317
  13.8 0.9 constant_dynamic-update-slice_fusion.1
  14.7 0.9 constant_dynamic-update-slice_fusion.refs_0_
  16.2 2.0 %collective-permute-done.3 = bf16[128,1024]{1,0:T(8,128)(2,1)} collective-permute-done((bf16[128,1024]{1,0:T(8,128)(2,1)S(1)}, bf16[128,1024]{1,0:T(8,128)(2,1)}, u32[]{:S(2)}, u32[]{:S(2)}) %collective-permute-start.3) | collective-permute-done | bytes 262176 | tf_op jit(solution)/shard_map/ppermute | solution.py:29
  18.2 1.0 broadcast_select_fusion.4
  19.2 1.2 %collective-permute-start.7 = (bf16[64,1024]{1,0:T(8,128)(2,1)S(1)}, bf16[64,1024]{1,0:T(8,128)(2,1)S(1)}, u32[]{:S(2)}, u32[]{:S(2)}) collective-permute-start(bf16[64,1024]{1,0:T(8,128)(2,1)S(1)} %get-tuple-element.514), channel_id=1, source_target_pairs={{0,2},{1,3},{2,0},{3,1},{4,6},{5,7},{6,4},{7,5},{8,10},{9,11},{10,... | collective-permute-start | bytes 393224 | tf_op jit(solution)/shard_map/ppermute | solution.py:29
  20.5 1.8 %broadcast_select_fusion = (bf16[64,7392]{1,0:T(8,128)(2,1)S(1)}, bf16[64,7392]{1,0:T(8,128)(2,1)S(1)}) fusion(bf16[64,7392]{1,0:T(8,128)(2,1)S(1)} %get-tuple-element.231, bf16[64,7392]{1,0:T(8,128)(2,1)} %collective-permute-done.2, pred[]{:T(512)S(6)} %eq.49, bf16[64,7392]{1,0:T(8,128)(2,1)S(1)} %get-tuple-element.230, ...), kind=kLoop, calls=%fused_computation.34 | loop fusion | flops 946176 | bytes 5677057 | tf_op jit(solution)/shard_map/jit(_where)/select_n | solution.py:48
  22.4 1.6 %collective-permute-start.6 = (bf16[32,7392]{1,0:T(8,128)(2,1)S(1)}, bf16[32,7392]{1,0:T(8,128)(2,1)S(1)}, u32[]{:S(2)}, u32[]{:S(2)}) collective-permute-start(bf16[32,7392]{1,0:T(8,128)(2,1)S(1)} %get-tuple-element.494), channel_id=1, source_target_pairs={{0,16},{4,20},{8,24},{12,28},{16,0},{20,4},{24,8},{28,12},{1,17},{... | collective-permute-start | bytes 1419272 | tf_op jit(solution)/shard_map/ppermute | solution.py:29
  24.0 1.6 %collective-permute-start.5 = (bf16[32,7392]{1,0:T(8,128)(2,1)S(1)}, bf16[32,7392]{1,0:T(8,128)(2,1)S(1)}, u32[]{:S(2)}, u32[]{:S(2)}) collective-permute-start(bf16[32,7392]{1,0:T(8,128)(2,1)S(1)} %get-tuple-element.496), channel_id=1, source_target_pairs={{0,8},{4,12},{8,0},{12,4},{16,24},{20,28},{24,16},{28,20},{1,9},{5... | collective-permute-start | bytes 1419272 | tf_op jit(solution)/shard_map/ppermute | solution.py:29
  25.6 4.0 %collective-permute-done.4.refs_1_ = bf16[192,1024]{1,0:T(8,128)(2,1)S(1)} collective-permute-done((bf16[192,1024]{1,0:T(8,128)(2,1)S(1)}, bf16[192,1024]{1,0:T(8,128)(2,1)S(1)}, u32[]{:S(2)}, u32[]{:S(2)}) %collective-permute-start.4) | collective-permute-done | bytes 393248 | tf_op jit(solution)/shard_map/ppermute | solution.py:29
  29.6 0.6 order_tokens.1.tok
  30.2 1.1 collective-permute-start.10
  31.4 1.6 %collective-permute-done.6 = bf16[32,7392]{1,0:T(8,128)(2,1)S(1)} collective-permute-done((bf16[32,7392]{1,0:T(8,128)(2,1)S(1)}, bf16[32,7392]{1,0:T(8,128)(2,1)S(1)}, u32[]{:S(2)}, u32[]{:S(2)}) %collective-permute-start.6) | collective-permute-done | bytes 473120 | tf_op jit(solution)/shard_map/ppermute | solution.py:29
  33.1 1.6 %collective-permute-start.9 = (bf16[16,7392]{1,0:T(8,128)(2,1)S(1)}, bf16[16,7392]{1,0:T(8,128)(2,1)S(1)}, u32[]{:S(2)}, u32[]{:S(2)}) collective-permute-start(bf16[16,7392]{1,0:T(8,128)(2,1)S(1)} %get-tuple-element.510), channel_id=1, source_target_pairs={{0,8},{4,12},{8,0},{12,4},{16,24},{20,28},{24,16},{28,20},{1,9},{5... | collective-permute-start | bytes 709640 | tf_op jit(solution)/shard_map/ppermute | solution.py:29
  34.7 1.0 collective-permute-done.5
  35.8 0.5 collective-permute-start.8
  36.4 7.0 %multiply.3 = (bf16[384,2560]{1,0:T(8,128)(2,1)S(1)}, f32[192,2560]{1,0:T(8,128)S(1)}, f32[192,2560]{1,0:T(8,128)S(1)}) custom-call(bf16[384,1024]{1,0:T(8,128)(2,1)S(1)} %order_tokens.1.tok, bf16[7392,1024]{1,0:T(8,128)(2,1)S(1)} %bitcast.28, bf16[7392,1024]{1,0:T(8,128)(2,1)} %bitcast.33), custom_call_target="tpu_custom_call" | custom-call | flops 17179869184 | bytes 33554432 | tf_op jit(solution)/shard_map/multiply/pallas_call | solution.py:118
  43.5 1.1 collective-permute-start.13
  44.7 2.1 %collective-permute-start.12 = (bf16[16,7392]{1,0:T(8,128)(2,1)S(1)}, bf16[16,7392]{1,0:T(8,128)(2,1)S(1)}, u32[]{:S(2)}, u32[]{:S(2)}) collective-permute-start(bf16[16,7392]{1,0:T(8,128)(2,1)S(1)} %broadcast_select_fusion.6), channel_id=1, source_target_pairs={{0,16},{4,20},{8,24},{12,28},{16,0},{20,4},{24,8},{28,12},{1,17},{... | collective-permute-start | bytes 709640 | tf_op jit(solution)/shard_map/ppermute | solution.py:29
  46.9 0.6 collective-permute-done.11
  48.1 1.1 collective-permute-start.15
  49.5 2.1 %collective-permute-start.16 = (bf16[96,2560]{1,0:T(8,128)(2,1)S(1)}, bf16[96,2560]{1,0:T(8,128)(2,1)S(1)}, u32[]{:S(2)}, u32[]{:S(2)}) collective-permute-start(bf16[96,2560]{1,0:T(8,128)(2,1)S(1)} %get-tuple-element.466), channel_id=1, source_target_pairs={{0,16},{4,20},{8,24},{12,28},{16,0},{20,4},{24,8},{28,12},{1,17},{... | collective-permute-start | bytes 1474568 | tf_op jit(solution)/shard_map/ppermute | solution.py:29
  51.5 6.9 %multiply.4 = (bf16[384,2560]{1,0:T(8,128)(2,1)S(1)}, f32[192,2560]{1,0:T(8,128)S(1)}, f32[192,2560]{1,0:T(8,128)S(1)}) custom-call(bf16[384,1024]{1,0:T(8,128)(2,1)S(1)} %order_tokens.1.tok, bf16[7392,1024]{1,0:T(8,128)(2,1)S(1)} %bitcast.29, bf16[7392,1024]{1,0:T(8,128)(2,1)} %bitcast.34), custom_call_target="tpu_custom_call" | custom-call | flops 17179869184 | bytes 33554432 | tf_op jit(solution)/shard_map/multiply/pallas_call | solution.py:118
  58.9 0.6 multiply_lower.1
  59.6 1.0 collective-permute-start.18
  60.7 7.0 %multiply.5 = (bf16[384,2560]{1,0:T(8,128)(2,1)S(1)}, f32[192,2560]{1,0:T(8,128)S(1)}, f32[192,2560]{1,0:T(8,128)S(1)}) custom-call(bf16[384,1024]{1,0:T(8,128)(2,1)S(1)} %order_tokens.1.tok, bf16[7392,1024]{1,0:T(8,128)(2,1)S(1)} %bitcast.30, bf16[7392,1024]{1,0:T(8,128)(2,1)} %bitcast.35), custom_call_target="tpu_custom_call" | custom-call | flops 17179869184 | bytes 33554432 | tf_op jit(solution)/shard_map/multiply/pallas_call | solution.py:118
  69.4 4.2 %collective-permute-done.19 = bf16[32,7392]{1,0:T(8,128)(2,1)S(1)} collective-permute-done((bf16[32,7392]{1,0:T(8,128)(2,1)S(1)}, bf16[32,7392]{1,0:T(8,128)(2,1)S(1)}, u32[]{:S(2)}, u32[]{:S(2)}) %collective-permute-start.19) | collective-permute-done | bytes 473120 | tf_op jit(solution)/shard_map/ppermute | solution.py:29
  74.0 0.6 collective-permute-start.20
  74.6 1.7 %collective-permute-start.23 = (bf16[144,2560]{1,0:T(8,128)(2,1)S(1)}, bf16[144,2560]{1,0:T(8,128)(2,1)S(1)}, u32[]{:S(2)}, u32[]{:S(2)}) collective-permute-start(bf16[144,2560]{1,0:T(8,128)(2,1)S(1)} %pad_maximum_fusion.1), channel_id=1, source_target_pairs={{0,16},{4,20},{8,24},{12,28},{16,0},{20,4},{24,8},{28,12},{1,17},{... | collective-permute-start | bytes 2211848 | tf_op jit(solution)/shard_map/ppermute | solution.py:29
  76.8 0.9 collective-permute-done.20.gate_c
  78.0 12.8 %merge.2 = (bf16[7392,1024]{1,0:T(8,128)(2,1)}, bf16[7392,1024]{1,0:T(8,128)(2,1)}) custom-call(bf16[256,1024]{1,0:T(8,128)(2,1)S(1)} %maximum_select_fusion.3.low, bf16[7392,1024]{1,0:T(8,128)(2,1)S(1)} %bitcast.31, bf16[7392,1024]{1,0:T(8,128)(2,1)} %bitcast.36, bf16[64,7392]{1,0:T(8,128)(2,1)S(1)} %maximum_select_fusion.gate_b, ...), custom_call_target="tpu_custom_call" | custom-call | flops 1024 | bytes 1024 | tf_op jit(solution)/shard_map/merge/pallas_call | solution.py:188
  90.7 2.3 %collective-permute-done.23.gate_came = bf16[144,2560]{1,0:T(8,128)(2,1)S(1)} collective-permute-done((bf16[144,2560]{1,0:T(8,128)(2,1)S(1)}, bf16[144,2560]{1,0:T(8,128)(2,1)S(1)}, u32[]{:S(2)}, u32[]{:S(2)}) %collective-permute-start.23) | collective-permute-done | bytes 737312 | tf_op jit(solution)/shard_map/ppermute | solution.py:29
  93.0 1.5 %collective-permute-done.22.up_came = bf16[144,2560]{1,0:T(8,128)(2,1)S(1)} collective-permute-done((bf16[144,2560]{1,0:T(8,128)(2,1)S(1)}, bf16[144,2560]{1,0:T(8,128)(2,1)S(1)}, u32[]{:S(2)}, u32[]{:S(2)}) %collective-permute-start.22) | collective-permute-done | bytes 737312 | tf_op jit(solution)/shard_map/ppermute | solution.py:29
  96.3 0.7 collective-permute-start.25
  97.1 10.7 %merge.3 = (bf16[7392,1024]{1,0:T(8,128)(2,1)}, bf16[7392,1024]{1,0:T(8,128)(2,1)}) custom-call(bf16[256,1024]{1,0:T(8,128)(2,1)S(1)} %maximum_select_fusion.3.low, bf16[7392,1024]{1,0:T(8,128)(2,1)S(1)} %bitcast.32, bf16[7392,1024]{1,0:T(8,128)(2,1)} %bitcast.37, ...), custom_call_target="tpu_custom_call", output_to_operand_aliasing={{0}: (7, {}), {1}: (8, {})} | custom-call | flops 1024 | bytes 1024 | tf_op jit(solution)/shard_map/merge/pallas_call | solution.py:188
  107.7 5.2 %collective-permute-done.26.gate_came = bf16[144,2560]{1,0:T(8,128)(2,1)S(1)} collective-permute-done((bf16[144,2560]{1,0:T(8,128)(2,1)S(1)}, bf16[144,2560]{1,0:T(8,128)(2,1)S(1)}, u32[]{:S(2)}, u32[]{:S(2)}) %collective-permute-start.26) | collective-permute-done | bytes 737312 | tf_op jit(solution)/shard_map/ppermute | solution.py:29
  112.9 0.8 collective-permute-done.25.up_came
  113.9 0.6 collective-permute-start.27
  114.7 1.5 %collective-permute-start.28 = (bf16[48,2560]{1,0:T(8,128)(2,1)S(1)}, bf16[48,2560]{1,0:T(8,128)(2,1)S(1)}, u32[]{:S(2)}, u32[]{:S(2)}) collective-permute-start(bf16[48,2560]{1,0:T(8,128)(2,1)S(1)} %get-tuple-element.472), channel_id=1, source_target_pairs={{0,16},{4,20},{8,24},{12,28},{16,0},{20,4},{24,8},{28,12},{1,17},{... | collective-permute-start | bytes 737288 | tf_op jit(solution)/shard_map/ppermute | solution.py:29
  116.6 1.2 finish.3.refs_0_
  117.8 1.2 finish.4.refs_0_
  119.0 1.2 collective-permute-done.27.up_came
  120.1 0.8 collective-permute-done.28.gate_came
  121.0 1.2 finish.5
  (86 shorter events, 8.6 us)
Async XLA Ops:
  0.6 14.1 %collective-permute-start = (bf16[96,1024]{1,0:T(8,128)(2,1)}, bf16[96,1024]{1,0:T(8,128)(2,1)}, u32[]{:S(2)}, u32[]{:S(2)}) collective-permute-start(bf16[96,1024]{1,0:T(8,128)(2,1)} %param.10), channel_id=1, source_target_pairs={{0,2},{1,3},{2,0},{3,1},{4,6},{5,7},{6,4},{7,5},{8,10},{9,11},{10,... | collective-permute-start | bytes 589832 | tf_op jit(solution)/shard_map/ppermute | solution.py:29
  7.2 11.0 %collective-permute-start.3 = (bf16[128,1024]{1,0:T(8,128)(2,1)S(1)}, bf16[128,1024]{1,0:T(8,128)(2,1)}, u32[]{:S(2)}, u32[]{:S(2)}) collective-permute-start(bf16[128,1024]{1,0:T(8,128)(2,1)S(1)} %get-tuple-element.491), channel_id=1, source_target_pairs={{0,1},{1,0},{2,3},{3,2},{4,5},{5,4},{6,7},{7,6},{8,9},{9,8},{10,11... | collective-permute-start | bytes 786440 | tf_op jit(solution)/shard_map/ppermute | solution.py:29
  10.5 3.1 %copy-start.1 = (s32[4]{0:T(128)S(1)}, s32[4]{0:T(128)}, u32[]{:S(2)}) copy-start(s32[4]{0:T(128)} %constant.91.clone) | copy-start | bytes 52
  10.5 10.0 %collective-permute-start.1 = (bf16[64,7392]{1,0:T(8,128)(2,1)S(1)}, bf16[64,7392]{1,0:T(8,128)(2,1)}, u32[]{:S(2)}, u32[]{:S(2)}) collective-permute-start(bf16[64,7392]{1,0:T(8,128)(2,1)S(1)} %get-tuple-element.489), channel_id=1, source_target_pairs={{0,4},{4,0},{8,12},{12,8},{16,20},{20,16},{24,28},{28,24},{1,5},{5... | collective-permute-start | bytes 2838536 | tf_op jit(solution)/shard_map/ppermute | solution.py:29
  13.1 7.4 %collective-permute-start.2 = (bf16[64,7392]{1,0:T(8,128)(2,1)}, bf16[64,7392]{1,0:T(8,128)(2,1)}, u32[]{:S(2)}, u32[]{:S(2)}) collective-permute-start(bf16[64,7392]{1,0:T(8,128)(2,1)} %get-tuple-element.487), channel_id=1, source_target_pairs={{0,4},{4,0},{8,12},{12,8},{16,20},{20,16},{24,28},{28,24},{1,5},{5... | collective-permute-start | bytes 2838536 | tf_op jit(solution)/shard_map/ppermute | solution.py:29
  15.7 13.9 %collective-permute-start.4 = (bf16[192,1024]{1,0:T(8,128)(2,1)S(1)}, bf16[192,1024]{1,0:T(8,128)(2,1)S(1)}, u32[]{:S(2)}, u32[]{:S(2)}) collective-permute-start(bf16[192,1024]{1,0:T(8,128)(2,1)S(1)} %constant_dynamic-update-slice_fusion.refs_0_), channel_id=1, source_target_pairs={{0,1},{1,0},{2,3},{3,2},{4,5},{5,4},{6,7},{7,6},{8,9},{9,8},{10,11... | collective-permute-start | bytes 1179656 | tf_op jit(solution)/shard_map/ppermute | solution.py:29
  19.2 11.0 %collective-permute-start.7 = (bf16[64,1024]{1,0:T(8,128)(2,1)S(1)}, bf16[64,1024]{1,0:T(8,128)(2,1)S(1)}, u32[]{:S(2)}, u32[]{:S(2)}) collective-permute-start(bf16[64,1024]{1,0:T(8,128)(2,1)S(1)} %get-tuple-element.514), channel_id=1, source_target_pairs={{0,2},{1,3},{2,0},{3,1},{4,6},{5,7},{6,4},{7,5},{8,10},{9,11},{10,... | collective-permute-start | bytes 393224 | tf_op jit(solution)/shard_map/ppermute | solution.py:29
  20.5 15.9 %copy-start = (bf16[1024,7392]{0,1:T(8,128)(2,1)S(1)}, bf16[1024,7392]{0,1:T(8,128)(2,1)}, u32[]{:S(2)}) copy-start(bf16[1024,7392]{0,1:T(8,128)(2,1)} %param.11) | copy-start | bytes 45416452
  22.4 10.6 %collective-permute-start.6 = (bf16[32,7392]{1,0:T(8,128)(2,1)S(1)}, bf16[32,7392]{1,0:T(8,128)(2,1)S(1)}, u32[]{:S(2)}, u32[]{:S(2)}) collective-permute-start(bf16[32,7392]{1,0:T(8,128)(2,1)S(1)} %get-tuple-element.494), channel_id=1, source_target_pairs={{0,16},{4,20},{8,24},{12,28},{16,0},{20,4},{24,8},{28,12},{1,17},{... | collective-permute-start | bytes 1419272 | tf_op jit(solution)/shard_map/ppermute | solution.py:29
  24.0 11.7 %collective-permute-start.5 = (bf16[32,7392]{1,0:T(8,128)(2,1)S(1)}, bf16[32,7392]{1,0:T(8,128)(2,1)S(1)}, u32[]{:S(2)}, u32[]{:S(2)}) collective-permute-start(bf16[32,7392]{1,0:T(8,128)(2,1)S(1)} %get-tuple-element.496), channel_id=1, source_target_pairs={{0,8},{4,12},{8,0},{12,4},{16,24},{20,28},{24,16},{28,20},{1,9},{5... | collective-permute-start | bytes 1419272 | tf_op jit(solution)/shard_map/ppermute | solution.py:29
  30.2 13.1 %collective-permute-start.10 = (bf16[64,1024]{1,0:T(8,128)(2,1)S(1)}, bf16[64,1024]{1,0:T(8,128)(2,1)S(1)}, u32[]{:S(2)}, u32[]{:S(2)}) collective-permute-start(bf16[64,1024]{1,0:T(8,128)(2,1)S(1)} %broadcast_select_fusion.7), channel_id=1, source_target_pairs={{0,2},{1,3},{2,0},{3,1},{4,6},{5,7},{6,4},{7,5},{8,10},{9,11},{10,... | collective-permute-start | bytes 393224 | tf_op jit(solution)/shard_map/ppermute | solution.py:29
  33.1 10.3 %collective-permute-start.9 = (bf16[16,7392]{1,0:T(8,128)(2,1)S(1)}, bf16[16,7392]{1,0:T(8,128)(2,1)S(1)}, u32[]{:S(2)}, u32[]{:S(2)}) collective-permute-start(bf16[16,7392]{1,0:T(8,128)(2,1)S(1)} %get-tuple-element.510), channel_id=1, source_target_pairs={{0,8},{4,12},{8,0},{12,4},{16,24},{20,28},{24,16},{28,20},{1,9},{5... | collective-permute-start | bytes 709640 | tf_op jit(solution)/shard_map/ppermute | solution.py:29
  35.8 7.6 %collective-permute-start.8 = (bf16[16,7392]{1,0:T(8,128)(2,1)S(1)}, bf16[16,7392]{1,0:T(8,128)(2,1)S(1)}, u32[]{:S(2)}, u32[]{:S(2)}) collective-permute-start(bf16[16,7392]{1,0:T(8,128)(2,1)S(1)} %get-tuple-element.512), channel_id=1, source_target_pairs={{0,16},{4,20},{8,24},{12,28},{16,0},{20,4},{24,8},{28,12},{1,17},{... | collective-permute-start | bytes 709640 | tf_op jit(solution)/shard_map/ppermute | solution.py:29
  43.4 4.0 %collective-permute-start.11 = (bf16[384,2560]{1,0:T(8,128)(2,1)S(1)}, bf16[384,2560]{1,0:T(8,128)(2,1)S(1)}, u32[]{:S(2)}, u32[]{:S(2)}) collective-permute-start(bf16[384,2560]{1,0:T(8,128)(2,1)S(1)} %get-tuple-element.257), channel_id=1, source_target_pairs={{0,4},{4,0},{8,12},{12,8},{16,20},{20,16},{24,28},{28,24},{1,5},{5... | collective-permute-start | bytes 5898248 | tf_op jit(solution)/shard_map/ppermute | solution.py:29
  43.5 14.9 %collective-permute-start.13 = (bf16[16,7392]{1,0:T(8,128)(2,1)S(1)}, bf16[16,7392]{1,0:T(8,128)(2,1)S(1)}, u32[]{:S(2)}, u32[]{:S(2)}) collective-permute-start(bf16[16,7392]{1,0:T(8,128)(2,1)S(1)} %broadcast_select_fusion.5), channel_id=1, source_target_pairs={{0,8},{4,12},{8,0},{12,4},{16,24},{20,28},{24,16},{28,20},{1,9},{5... | collective-permute-start | bytes 709640 | tf_op jit(solution)/shard_map/ppermute | solution.py:29
  44.7 13.8 %collective-permute-start.12 = (bf16[16,7392]{1,0:T(8,128)(2,1)S(1)}, bf16[16,7392]{1,0:T(8,128)(2,1)S(1)}, u32[]{:S(2)}, u32[]{:S(2)}) collective-permute-start(bf16[16,7392]{1,0:T(8,128)(2,1)S(1)} %broadcast_select_fusion.6), channel_id=1, source_target_pairs={{0,16},{4,20},{8,24},{12,28},{16,0},{20,4},{24,8},{28,12},{1,17},{... | collective-permute-start | bytes 709640 | tf_op jit(solution)/shard_map/ppermute | solution.py:29
  46.8 11.7 %collective-permute-start.14 = (bf16[128,1024]{1,0:T(8,128)(2,1)S(1)}, bf16[128,1024]{1,0:T(8,128)(2,1)S(1)}, u32[]{:S(2)}, u32[]{:S(2)}) collective-permute-start(bf16[128,1024]{1,0:T(8,128)(2,1)S(1)} %maximum_select_fusion.6), channel_id=1, source_target_pairs={{0,1},{1,0},{2,3},{3,2},{4,5},{5,4},{6,7},{7,6},{8,9},{9,8},{10,11... | collective-permute-start | bytes 786440 | tf_op jit(solution)/shard_map/ppermute | solution.py:29
  48.1 19.5 %collective-permute-start.15 = (bf16[96,2560]{1,0:T(8,128)(2,1)S(1)}, bf16[96,2560]{1,0:T(8,128)(2,1)S(1)}, u32[]{:S(2)}, u32[]{:S(2)}) collective-permute-start(bf16[96,2560]{1,0:T(8,128)(2,1)S(1)} %get-tuple-element.468), channel_id=1, source_target_pairs={{0,8},{4,12},{8,0},{12,4},{16,24},{20,28},{24,16},{28,20},{1,9},{5... | collective-permute-start | bytes 1474568 | tf_op jit(solution)/shard_map/ppermute | solution.py:29
  49.5 18.5 %collective-permute-start.16 = (bf16[96,2560]{1,0:T(8,128)(2,1)S(1)}, bf16[96,2560]{1,0:T(8,128)(2,1)S(1)}, u32[]{:S(2)}, u32[]{:S(2)}) collective-permute-start(bf16[96,2560]{1,0:T(8,128)(2,1)S(1)} %get-tuple-element.466), channel_id=1, source_target_pairs={{0,16},{4,20},{8,24},{12,28},{16,0},{20,4},{24,8},{28,12},{1,17},{... | collective-permute-start | bytes 1474568 | tf_op jit(solution)/shard_map/ppermute | solution.py:29
  58.7 14.9 %collective-permute-start.19 = (bf16[32,7392]{1,0:T(8,128)(2,1)S(1)}, bf16[32,7392]{1,0:T(8,128)(2,1)S(1)}, u32[]{:S(2)}, u32[]{:S(2)}) collective-permute-start(bf16[32,7392]{1,0:T(8,128)(2,1)S(1)} %maximum_select_fusion.5), channel_id=1, source_target_pairs={{0,16},{4,20},{8,24},{12,28},{16,0},{20,4},{24,8},{28,12},{1,17},{... | collective-permute-start | bytes 1419272 | tf_op jit(solution)/shard_map/ppermute | solution.py:29
  59.5 8.5 %collective-permute-start.17 = (bf16[384,2560]{1,0:T(8,128)(2,1)S(1)}, bf16[384,2560]{1,0:T(8,128)(2,1)S(1)}, u32[]{:S(2)}, u32[]{:S(2)}) collective-permute-start(bf16[384,2560]{1,0:T(8,128)(2,1)S(1)} %get-tuple-element.316), channel_id=1, source_target_pairs={{0,4},{4,0},{8,12},{12,8},{16,20},{20,16},{24,28},{28,24},{1,5},{5... | collective-permute-start | bytes 5898248 | tf_op jit(solution)/shard_map/ppermute | solution.py:29
  59.6 14.0 %collective-permute-start.18 = (bf16[32,7392]{1,0:T(8,128)(2,1)S(1)}, bf16[32,7392]{1,0:T(8,128)(2,1)S(1)}, u32[]{:S(2)}, u32[]{:S(2)}) collective-permute-start(bf16[32,7392]{1,0:T(8,128)(2,1)S(1)} %maximum_select_fusion.4), channel_id=1, source_target_pairs={{0,8},{4,12},{8,0},{12,4},{16,24},{20,28},{24,16},{28,20},{1,9},{5... | collective-permute-start | bytes 1419272 | tf_op jit(solution)/shard_map/ppermute | solution.py:29
  67.7 23.0 %collective-permute-start.24 = (bf16[384,2560]{1,0:T(8,128)(2,1)S(1)}, bf16[384,2560]{1,0:T(8,128)(2,1)S(1)}, u32[]{:S(2)}, u32[]{:S(2)}) collective-permute-start(bf16[384,2560]{1,0:T(8,128)(2,1)S(1)} %get-tuple-element.373), channel_id=1, source_target_pairs={{0,4},{4,0},{8,12},{12,8},{16,20},{20,16},{24,28},{28,24},{1,5},{5... | collective-permute-start | bytes 5898248 | tf_op jit(solution)/shard_map/ppermute | solution.py:29
  73.8 3.1 %collective-permute-start.21 = (bf16[64,7392]{1,0:T(8,128)(2,1)S(1)}, bf16[64,7392]{1,0:T(8,128)(2,1)S(1)}, u32[]{:S(2)}, u32[]{:S(2)}) collective-permute-start(bf16[64,7392]{1,0:T(8,128)(2,1)S(1)} %maximum_select_fusion.1.up_b), channel_id=1, source_target_pairs={{0,4},{4,0},{8,12},{12,8},{16,20},{20,16},{24,28},{28,24},{1,5},{5... | collective-permute-start | bytes 2838536 | tf_op jit(solution)/shard_map/ppermute | solution.py:29
  74.0 3.7 %collective-permute-start.20 = (bf16[64,7392]{1,0:T(8,128)(2,1)S(1)}, bf16[64,7392]{1,0:T(8,128)(2,1)S(1)}, u32[]{:S(2)}, u32[]{:S(2)}) collective-permute-start(bf16[64,7392]{1,0:T(8,128)(2,1)S(1)} %maximum_select_fusion.gate_b), channel_id=1, source_target_pairs={{0,4},{4,0},{8,12},{12,8},{16,20},{20,16},{24,28},{28,24},{1,5},{5... | collective-permute-start | bytes 2838536 | tf_op jit(solution)/shard_map/ppermute | solution.py:29
  74.6 18.5 %collective-permute-start.23 = (bf16[144,2560]{1,0:T(8,128)(2,1)S(1)}, bf16[144,2560]{1,0:T(8,128)(2,1)S(1)}, u32[]{:S(2)}, u32[]{:S(2)}) collective-permute-start(bf16[144,2560]{1,0:T(8,128)(2,1)S(1)} %pad_maximum_fusion.1), channel_id=1, source_target_pairs={{0,16},{4,20},{8,24},{12,28},{16,0},{20,4},{24,8},{28,12},{1,17},{... | collective-permute-start | bytes 2211848 | tf_op jit(solution)/shard_map/ppermute | solution.py:29
  76.3 18.2 %collective-permute-start.22 = (bf16[144,2560]{1,0:T(8,128)(2,1)S(1)}, bf16[144,2560]{1,0:T(8,128)(2,1)S(1)}, u32[]{:S(2)}, u32[]{:S(2)}) collective-permute-start(bf16[144,2560]{1,0:T(8,128)(2,1)S(1)} %pad_maximum_fusion), channel_id=1, source_target_pairs={{0,8},{4,12},{8,0},{12,4},{16,24},{20,28},{24,16},{28,20},{1,9},{5... | collective-permute-start | bytes 2211848 | tf_op jit(solution)/shard_map/ppermute | solution.py:29
  95.5 17.4 %collective-permute-start.26 = (bf16[144,2560]{1,0:T(8,128)(2,1)S(1)}, bf16[144,2560]{1,0:T(8,128)(2,1)S(1)}, u32[]{:S(2)}, u32[]{:S(2)}) collective-permute-start(bf16[144,2560]{1,0:T(8,128)(2,1)S(1)} %pad_maximum_fusion.3), channel_id=1, source_target_pairs={{0,16},{4,20},{8,24},{12,28},{16,0},{20,4},{24,8},{28,12},{1,17},{... | collective-permute-start | bytes 2211848 | tf_op jit(solution)/shard_map/ppermute | solution.py:29
  96.3 17.3 %collective-permute-start.25 = (bf16[144,2560]{1,0:T(8,128)(2,1)S(1)}, bf16[144,2560]{1,0:T(8,128)(2,1)S(1)}, u32[]{:S(2)}, u32[]{:S(2)}) collective-permute-start(bf16[144,2560]{1,0:T(8,128)(2,1)S(1)} %pad_maximum_fusion.2), channel_id=1, source_target_pairs={{0,8},{4,12},{8,0},{12,4},{16,24},{20,28},{24,16},{28,20},{1,9},{5... | collective-permute-start | bytes 2211848 | tf_op jit(solution)/shard_map/ppermute | solution.py:29
  113.9 6.3 %collective-permute-start.27 = (bf16[48,2560]{1,0:T(8,128)(2,1)S(1)}, bf16[48,2560]{1,0:T(8,128)(2,1)S(1)}, u32[]{:S(2)}, u32[]{:S(2)}) collective-permute-start(bf16[48,2560]{1,0:T(8,128)(2,1)S(1)} %get-tuple-element.470), channel_id=1, source_target_pairs={{0,8},{4,12},{8,0},{12,4},{16,24},{20,28},{24,16},{28,20},{1,9},{5... | collective-permute-start | bytes 737288 | tf_op jit(solution)/shard_map/ppermute | solution.py:29
  114.7 6.3 %collective-permute-start.28 = (bf16[48,2560]{1,0:T(8,128)(2,1)S(1)}, bf16[48,2560]{1,0:T(8,128)(2,1)S(1)}, u32[]{:S(2)}, u32[]{:S(2)}) collective-permute-start(bf16[48,2560]{1,0:T(8,128)(2,1)S(1)} %get-tuple-element.472), channel_id=1, source_target_pairs={{0,16},{4,20},{8,24},{12,28},{16,0},{20,4},{24,8},{28,12},{1,17},{... | collective-permute-start | bytes 737288 | tf_op jit(solution)/shard_map/ppermute | solution.py:29
